TPU v7x, 32 devices: a whole 2x2x4 slice. The times are simulated.
32 devices in a mesh: grp: 2 (over x), blade: 8 (over z, y), dof: 2 (over core).
Axes of the slice: x: 2, y: 2, z: 4, core: 2. Of those that a mesh axis runs over, the one named last changes fastest.
Arguments:
- panel: bfloat16 [8192, 512], P(('grp', 'blade', 'dof')), parts along dimension 0, may hold values from -0.25 to 0.25
- stiffness: bfloat16 [96, 64, 128, 128], P(('grp', 'blade'), 'dof'), parts along dimension 0, may hold values from -0.5 to 0.5
- block_rows: int32 [96, 64], P(('grp', 'blade'), 'dof'), parts along dimension 0, may hold values from 0 to 31
- block_cols: int32 [96, 64], P(('grp', 'blade'), 'dof'), parts along dimension 0, may hold values from 0 to 31
Outputs:
- spectral: float32 [2, 96, 512, 512], P(None, ('grp', 'blade'), 'dof'), parts along dimension 1
There are 2 independent parts, one for each index of `grp`. A program takes and returns all parts, laid end to end along the dimension named above; each array names one. Nothing has to cross between parts.
Inputs may be any that keep to these rules, and one draw needn't show every extreme that they name: `block_rows`: row block index of each stiffness block; indices of one blade may repeat. `block_cols`: column block index of each stiffness block; indices of one blade may repeat.
All inputs are finite; a program needn't handle non-finite values.
Results may differ from a plain program's by a relative error of at most 0.0029.
Values may be sent and summed in bfloat16 or wider, within the bound.
A program may use at most 128 MiB of HBM per device.

v0:
```python
import math

import jax
import jax.numpy as jnp
from jax import lax
from jax.sharding import PartitionSpec as P


def body(panel, stiffness, block_rows, block_cols):
    block_size = stiffness.shape[-1]
    modes = panel.shape[-1]
    whole = lax.all_gather(panel, ("blade", "dof"), axis=0, tiled=True)
    blocks = whole.reshape(-1, block_size, modes)

    def one_blade(items):
        mats, rows, cols = items
        chosen = jnp.take(blocks, cols, axis=0)
        image = jnp.einsum("nij,njm->nim", mats, chosen, preferred_element_type=jnp.float32)
        image = image.astype(jnp.bfloat16)
        left = jnp.take(blocks, rows, axis=0).reshape(-1, modes)
        return lax.dot_general(
            left,
            image.reshape(-1, modes),
            (((0,), (0,)), ((), ())),
            preferred_element_type=jnp.float32,
        )

    partial_proj = lax.map(one_blade, (stiffness, block_rows, block_cols))
    blade_count = stiffness.shape[0] * lax.axis_size("blade")
    index = jnp.arange(blade_count, dtype=jnp.int32)
    angle = (index[:, None] * index[None, :] % blade_count).astype(jnp.float32) * (
        2.0 * math.pi / blade_count
    )
    cosine = jnp.cos(angle)
    sine = jnp.sin(angle)
    stacked = lax.all_to_all(partial_proj, "blade", split_axis=1, concat_axis=0, tiled=True)
    real_part = jnp.einsum("hb,brc->hrc", cosine, stacked, precision=lax.Precision.HIGHEST)
    imag_part = -jnp.einsum("hb,brc->hrc", sine, stacked, precision=lax.Precision.HIGHEST)
    joined = jnp.stack([real_part, imag_part])
    full_spec = lax.all_to_all(joined, "blade", split_axis=1, concat_axis=2, tiled=True)
    result = lax.psum_scatter(full_spec, "dof", scatter_dimension=2, tiled=True)
    return result


def solution(mesh):
    placed = (
        P(("grp", "blade", "dof"), None),
        P(("grp", "blade"), "dof", None, None),
        P(("grp", "blade"), "dof"),
        P(("grp", "blade"), "dof"),
    )
    return jax.shard_map(
        body,
        mesh=mesh,
        in_specs=placed,
        out_specs=P(None, ("grp", "blade"), "dof", None),
        check_vma=False,
    )
```

profile of v0, /device:TPU:0, one launch (start us, length us, event | category | flops | bytes accessed | tf_op | source)
XLA Modules:
  0.0 863.4 jit_solution(7075036304253567163)
XLA Ops:
  6.5 0.7 all-gather.2.cloned.1.call-update
  7.3 55.5 %all-gather.2.cloned.1.call-done = bf16[4096,512]{1,0:T(8,128)(2,1)} async-done(((bf16[256,512]{1,0:T(8,128)(2,1)}), bf16[4096,512]{1,0:T(8,128)(2,1)}) %all-gather.2.cloned.1.call-update) | async-done | bytes 4194320 | tf_op jit(solution)/shard_map/all_gather | solution.py:12
  62.8 244.8 %while.10 = (s32[]{:T(128)}, f32[6,512,512]{2,0,1:T(8,128)}, s32[6,32]{1,0:T(8,128)}, bf16[32,128,512]{2,1,0:T(8,128)(2,1)}, bf16[6,32,128,128]{3,2,1,0:T(8,128)...) while((s32[]{:T(128)}, f32[6,512,512]{2,0,1:T(8,128)}, s32[6,32]{1,0:T(8,128)}, ...), condition=%wide.region_1.3_spmd, body=%wide.region_0.2_spmd.sunk | while | flops 2690648576 | bytes 31466728 | solution.py:28
  62.8 0.7 compare_and_fusion.3
  63.5 4.9 gather_fusion.1
  68.5 5.0 gather_fusion
  73.5 7.2 fusion.71
  80.8 1.1 copy.41
  81.8 21.8 %dynamic_update_slice.5 = f32[6,512,512]{2,0,1:T(8,128)} dynamic-update-slice(f32[6,512,512]{2,0,1:T(8,128)} %get-tuple-element.111, f32[1,512,512]{2,0,1:T(1,128)S(1)} %copy.41, s32[]{:T(128)S(6)} %copy.45, s32[]{:T(128)} %constant.36.clone.1..sunk, s32[]{:T(128)} %constant.36.clone.1..sunk) | dynamic-update-slice | bytes 2097156 | tf_op jit(solution)/shard_map/while/body/jit(dynamic_update_index_in_dim)/dynamic_update_slice | solution.py:28
  103.6 0.7 compare_and_fusion.3
  104.3 4.9 gather_fusion.1
  109.3 5.0 gather_fusion
  114.3 7.2 fusion.71
  121.6 1.1 copy.41
  122.6 21.8 %dynamic_update_slice.5 = f32[6,512,512]{2,0,1:T(8,128)} dynamic-update-slice(f32[6,512,512]{2,0,1:T(8,128)} %get-tuple-element.111, f32[1,512,512]{2,0,1:T(1,128)S(1)} %copy.41, s32[]{:T(128)S(6)} %copy.45, s32[]{:T(128)} %constant.36.clone.1..sunk, s32[]{:T(128)} %constant.36.clone.1..sunk) | dynamic-update-slice | bytes 2097156 | tf_op jit(solution)/shard_map/while/body/jit(dynamic_update_index_in_dim)/dynamic_update_slice | solution.py:28
  144.4 0.7 compare_and_fusion.3
  145.1 4.9 gather_fusion.1
  150.1 5.0 gather_fusion
  155.1 7.2 fusion.71
  162.3 1.1 copy.41
  163.4 21.8 %dynamic_update_slice.5 = f32[6,512,512]{2,0,1:T(8,128)} dynamic-update-slice(f32[6,512,512]{2,0,1:T(8,128)} %get-tuple-element.111, f32[1,512,512]{2,0,1:T(1,128)S(1)} %copy.41, s32[]{:T(128)S(6)} %copy.45, s32[]{:T(128)} %constant.36.clone.1..sunk, s32[]{:T(128)} %constant.36.clone.1..sunk) | dynamic-update-slice | bytes 2097156 | tf_op jit(solution)/shard_map/while/body/jit(dynamic_update_index_in_dim)/dynamic_update_slice | solution.py:28
  185.2 0.7 compare_and_fusion.3
  185.9 4.9 gather_fusion.1
  190.9 5.0 gather_fusion
  195.9 7.2 fusion.71
  203.1 1.1 copy.41
  204.2 21.8 %dynamic_update_slice.5 = f32[6,512,512]{2,0,1:T(8,128)} dynamic-update-slice(f32[6,512,512]{2,0,1:T(8,128)} %get-tuple-element.111, f32[1,512,512]{2,0,1:T(1,128)S(1)} %copy.41, s32[]{:T(128)S(6)} %copy.45, s32[]{:T(128)} %constant.36.clone.1..sunk, s32[]{:T(128)} %constant.36.clone.1..sunk) | dynamic-update-slice | bytes 2097156 | tf_op jit(solution)/shard_map/while/body/jit(dynamic_update_index_in_dim)/dynamic_update_slice | solution.py:28
  226.0 0.7 compare_and_fusion.3
  226.7 4.9 gather_fusion.1
  231.7 5.0 gather_fusion
  236.7 7.2 fusion.71
  243.9 1.1 copy.41
  245.0 21.8 %dynamic_update_slice.5 = f32[6,512,512]{2,0,1:T(8,128)} dynamic-update-slice(f32[6,512,512]{2,0,1:T(8,128)} %get-tuple-element.111, f32[1,512,512]{2,0,1:T(1,128)S(1)} %copy.41, s32[]{:T(128)S(6)} %copy.45, s32[]{:T(128)} %constant.36.clone.1..sunk, s32[]{:T(128)} %constant.36.clone.1..sunk) | dynamic-update-slice | bytes 2097156 | tf_op jit(solution)/shard_map/while/body/jit(dynamic_update_index_in_dim)/dynamic_update_slice | solution.py:28
  266.8 0.7 compare_and_fusion.3
  267.5 4.9 gather_fusion.1
  272.5 5.0 gather_fusion
  277.5 7.2 fusion.71
  284.7 1.1 copy.41
  285.8 21.8 %dynamic_update_slice.5 = f32[6,512,512]{2,0,1:T(8,128)} dynamic-update-slice(f32[6,512,512]{2,0,1:T(8,128)} %get-tuple-element.111, f32[1,512,512]{2,0,1:T(1,128)S(1)} %copy.41, s32[]{:T(128)S(6)} %copy.45, s32[]{:T(128)} %constant.36.clone.1..sunk, s32[]{:T(128)} %constant.36.clone.1..sunk) | dynamic-update-slice | bytes 2097156 | tf_op jit(solution)/shard_map/while/body/jit(dynamic_update_index_in_dim)/dynamic_update_slice | solution.py:28
  307.6 187.5 %all_to_all.36 = f32[6,512,512]{2,0,1:T(8,128)S(1)} all-to-all(f32[6,512,512]{2,0,1:T(8,128)} %get-tuple-element.38), channel_id=1, replica_groups=mesh['grp'=2,'blade'=8,'dof'=2] {'blade'}, dimensions={1} | all-to-all | bytes 12582912 | tf_op jit(solution)/shard_map/all_to_all | solution.py:36
  495.1 3.6 copy.21
  498.6 9.7 %negate_bitcast_fusion = f32[1,48,64,512]{3,1,2,0:T(8,128)S(1)} fusion(f32[48,64,512]{2,1,0:T(8,128)S(1)} %bitcast.41), kind=kOutput, calls=%fused_computation.26 | convolution fusion | flops 907563264 | bytes 12582912 | tf_op jit(solution)/shard_map/hb,brc->hrc/dot_general | solution.py:38
  508.3 10.2 %fusion.34 = f32[1,48,64,512]{3,1,2,0:T(8,128)} fusion(f32[48,64,512]{2,1,0:T(8,128)S(1)} %bitcast.42), kind=kOutput, calls=%fused_computation.31 | convolution fusion | flops 905990400 | bytes 12582912 | tf_op jit(solution)/shard_map/hb,brc->hrc/dot_general | solution.py:37
  518.5 9.5 %pad_maximum_fusion = f32[2,48,64,512]{3,1,2,0:T(8,128)} fusion(f32[1,48,64,512]{3,1,2,0:T(8,128)S(1)} %negate_bitcast_fusion, f32[1,48,64,512]{3,1,2,0:T(8,128)} %fusion.34), kind=kLoop, calls=%fused_computation.25 | loop fusion | flops 3145728 | bytes 25165824 | tf_op jit(solution)/shard_map/stack | solution.py:39
  528.0 16.4 %copy.24 = f32[2,48,64,512]{3,2,0,1:T(8,128)} copy(f32[2,48,64,512]{3,1,2,0:T(8,128)} %pad_maximum_fusion) | data formatting | bytes 25165824 | tf_op jit(solution)/shard_map/stack | solution.py:39
  544.4 279.6 %all_to_all.37 = f32[2,48,64,512]{3,2,0,1:T(8,128)} all-to-all(f32[2,48,64,512]{3,2,0,1:T(8,128)} %copy.24), channel_id=1, replica_groups=mesh['grp'=2,'blade'=8,'dof'=2] {'blade'}, dimensions={1} | all-to-all | bytes 25165824 | tf_op jit(solution)/shard_map/all_to_all | solution.py:40
  823.9 12.0 %copy.26 = f32[2,6,8,64,512]{4,3,2,1,0:T(8,128)} copy(f32[2,6,8,64,512]{4,3,0,1,2:T(8,128)} %bitcast.44) | data formatting | bytes 25165824 | tf_op jit(solution)/shard_map/all_to_all | solution.py:40
  835.9 20.6 %reduce-scatter.2.cloned.1.call-done = f32[2,6,256,512]{3,2,1,0:T(8,128)} async-done(((f32[2,6,512,512]{3,2,1,0:T(8,128)}), f32[2,6,256,512]{3,2,1,0:T(8,128)}) %reduce-scatter.2.cloned.1.call-update) | async-done | bytes 6291472 | tf_op jit(solution)/shard_map/reduce_scatter | solution.py:41
  (16 shorter events, 0.1 us)
Async XLA Ops:
  6.5 56.3 %all-gather.2.cloned.1.call-start = ((), (), s32[]{:S(2)}) async-start(), calls=%async_computation.3 | async-start | bytes 4456448 | tf_op jit(solution)/shard_map/all_gather | solution.py:12
  7.3 849.3 %reduce-scatter.2.cloned.1.call-start = ((), (), s32[]{:S(2)}) async-start(), calls=%async_computation.4 | async-start | bytes 18874368 | tf_op jit(solution)/shard_map/reduce_scatter | solution.py:41
Sparse Core Ops, SparseCore 0:
  9.5 53.2 all-gather.1
  836.0 20.4 reduce-scatter.1
where the time goes:
time: 868 us; the launch traced here: 863 us
  blocking collectives  467 us (54%)
  local copies, waits for them, and re-layouts  229 us (26%)
  waiting for transfers between devices  76.9 us (9%)
  matrix products  63.3 us (7%)
  other arithmetic  13.8 us (2%)
  between operations  13.4 us (2%)
    all_to_all x1, blocking collectives, body(): lax.all_to_all(joined, 'blade', split_axis=1, concat_axis=2, tiled=True)  280 us
    all_to_all x1, blocking collectives, body(): lax.all_to_all(partial_proj, 'blade', split_axis=1, concat_axis=0, tiled=...  187 us
    dynamic_update_slice x12, local copies, waits for them, and re-layouts, body(): partial_proj = lax.map(one_blade, (stiffness, block_rows, block_cols))  137 us
    all_gather x1, waiting for transfers between devices, body(): whole = lax.all_gather(panel, ('blade', 'dof'), axis=0, tiled=True)  55.5 us
    dot_general x6, matrix products, one_blade(): lax.dot_general(left, image.reshape(-1, modes), (((0,), (0,)), ((), ())),...  43.5 us
    gather x6, local copies, waits for them, and re-layouts, one_blade(): chosen = jnp.take(blocks, cols, axis=0)  30.1 us
    gather x6, local copies, waits for them, and re-layouts, one_blade(): left = jnp.take(blocks, rows, axis=0).reshape(-1, modes)  29.7 us
    reduce_scatter x1, waiting for transfers between devices, body(): result = lax.psum_scatter(full_spec, 'dof', scatter_dimension=2, tiled=True)  20.6 us
  transfers between devices with their start and end apart: 2, of which 2 were waited for; matrix products, arithmetic and copies ran while one was open for 0% of the time, Pallas kernels for 0%

commit v1 on v0

--- a/solution.py
+++ b/solution.py
@@ -26,20 +26,20 @@
         )
 
     partial_proj = lax.map(one_blade, (stiffness, block_rows, block_cols))
+    half = lax.psum_scatter(partial_proj, "dof", scatter_dimension=1, tiled=True)
+    half = half.astype(jnp.bfloat16)
     blade_count = stiffness.shape[0] * lax.axis_size("blade")
     index = jnp.arange(blade_count, dtype=jnp.int32)
     angle = (index[:, None] * index[None, :] % blade_count).astype(jnp.float32) * (
         2.0 * math.pi / blade_count
     )
-    cosine = jnp.cos(angle)
-    sine = jnp.sin(angle)
-    stacked = lax.all_to_all(partial_proj, "blade", split_axis=1, concat_axis=0, tiled=True)
-    real_part = jnp.einsum("hb,brc->hrc", cosine, stacked, precision=lax.Precision.HIGHEST)
-    imag_part = -jnp.einsum("hb,brc->hrc", sine, stacked, precision=lax.Precision.HIGHEST)
-    joined = jnp.stack([real_part, imag_part])
+    table = jnp.stack([jnp.cos(angle), -jnp.sin(angle)])
+    stacked = lax.all_to_all(half, "blade", split_axis=1, concat_axis=0, tiled=True)
+    joined = jnp.einsum(
+        "phb,brc->phrc", table, stacked.astype(jnp.float32), precision=lax.Precision.HIGHEST
+    ).astype(jnp.bfloat16)
     full_spec = lax.all_to_all(joined, "blade", split_axis=1, concat_axis=2, tiled=True)
-    result = lax.psum_scatter(full_spec, "dof", scatter_dimension=2, tiled=True)
-    return result
+    return full_spec.astype(jnp.float32)
 
 
 def solution(mesh):

time: 868 us -> 476 us (0.55)
  blocking collectives: 467 us -> 74.3 us
  waiting for transfers between devices: 76.9 us -> 120 us
  local copies, waits for them, and re-layouts: 229 us -> 203 us
  matrix products: 63.3 us -> 46.3 us
    all_to_all x1, blocking collectives: 280 us -> 74.3 us  [body(): lax.all_to_all(joined, 'blade', split_axis=1, concat_axis=2, tiled=True)]
    all_to_all x1 -> x0, blocking collectives: 187 us -> none  [body(): lax.all_to_all(partial_proj, 'blade', split_axis=1, concat_axis=0, tiled=...]
    all_to_all x0 -> x1, waiting for transfers between devices: none -> 48.5 us  [body(): lax.all_to_all(half, 'blade', split_axis=1, concat_axis=0, tiled=True)]
    dot_general x2 -> x1, matrix products: 19.9 us -> 2.86 us  [body(): jnp.einsum('phb,brc->phrc', table, stacked.astype(jnp.float32), precision...]
    another operation x1 -> x0, local copies, waits for them, and re-layouts: 16.4 us -> none  [body(): joined = jnp.stack([real_part, imag_part])]
    all_to_all x1, local copies, waits for them, and re-layouts: 12 us -> 0.4 us  [body(): lax.all_to_all(joined, 'blade', split_axis=1, concat_axis=2, tiled=True)]
    another operation x1 -> x0, other arithmetic: 9.46 us -> none  [body(): joined = jnp.stack([real_part, imag_part])]
  transfers between devices with their start and end apart: 2 -> 3, of which waited for: 2 -> 3; matrix products, arithmetic and copies ran while one was open for 0% -> 0% of each run, Pallas kernels for 0% -> 0%
where the time goes in v1:
time: 476 us; the launch traced here: 472 us
  local copies, waits for them, and re-layouts  203 us (43%)
  waiting for transfers between devices  120 us (25%)
  blocking collectives  74.3 us (16%)
  matrix products  46.3 us (10%)
  between operations  13.4 us (3%)
  other arithmetic  9.17 us (2%)
  starting transfers between devices  5.9 us (1%)
    dynamic_update_slice x12, local copies, waits for them, and re-layouts, body(): partial_proj = lax.map(one_blade, (stiffness, block_rows, block_cols))  137 us
    all_to_all x1, blocking collectives, body(): lax.all_to_all(joined, 'blade', split_axis=1, concat_axis=2, tiled=True)  74.3 us
    all_gather x1, waiting for transfers between devices, body(): whole = lax.all_gather(panel, ('blade', 'dof'), axis=0, tiled=True)  55.5 us
    all_to_all x1, waiting for transfers between devices, body(): lax.all_to_all(half, 'blade', split_axis=1, concat_axis=0, tiled=True)  48.5 us
    dot_general x6, matrix products, one_blade(): lax.dot_general(left, image.reshape(-1, modes), (((0,), (0,)), ((), ())),...  43.5 us
    gather x6, local copies, waits for them, and re-layouts, one_blade(): chosen = jnp.take(blocks, cols, axis=0)  30.1 us
    gather x6, local copies, waits for them, and re-layouts, one_blade(): left = jnp.take(blocks, rows, axis=0).reshape(-1, modes)  29.6 us
    reduce_scatter x1, waiting for transfers between devices, body(): lax.psum_scatter(partial_proj, 'dof', scatter_dimension=1, tiled=True)  15.5 us
  transfers between devices with their start and end apart: 3, of which 3 were waited for; matrix products, arithmetic and copies ran while one was open for 0% of the time, Pallas kernels for 0%

profile of v1, /device:TPU:0, one launch (start us, length us, event | category | flops | bytes accessed | tf_op | source)
XLA Modules:
  0.0 472.1 jit_solution(11399360816654444198)
XLA Ops:
  6.5 0.7 all-gather.2.cloned.1.call-update
  7.3 55.5 %all-gather.2.cloned.1.call-done = bf16[4096,512]{1,0:T(8,128)(2,1)} async-done(((bf16[256,512]{1,0:T(8,128)(2,1)}), bf16[4096,512]{1,0:T(8,128)(2,1)}) %all-gather.2.cloned.1.call-update) | async-done | bytes 4194320 | tf_op jit(solution)/shard_map/all_gather | solution.py:12
  62.8 244.5 %while.10 = (s32[]{:T(128)}, f32[6,512,512]{2,0,1:T(8,128)}, s32[6,32]{1,0:T(8,128)}, bf16[32,128,512]{2,1,0:T(8,128)(2,1)}, bf16[6,32,128,128]{3,2,1,0:T(8,128)...) while((s32[]{:T(128)}, f32[6,512,512]{2,0,1:T(8,128)}, s32[6,32]{1,0:T(8,128)}, ...), condition=%wide.region_1.3_spmd, body=%wide.region_0.2_spmd.sunk | while | flops 2690648576 | bytes 31466728 | solution.py:28
  62.8 0.7 compare_and_fusion.3
  63.5 5.0 %gather_fusion = bf16[32,128,512]{2,1,0:T(8,128)(2,1)} fusion(bf16[32,128,512]{2,1,0:T(8,128)(2,1)} %get-tuple-element.123, s32[1024]{0:T(1024)S(1)} %pad_clamp_fusion.4), kind=kCustom, calls=%fused_computation.1.clone.clone.1 | custom fusion | bytes 8388736 | tf_op jit(solution)/shard_map/while/body/eval_jaxpr/jit(_take)/gather | solution.py:17
  68.6 4.9 %gather_fusion.1 = bf16[32,128,512]{2,1,0:T(8,128)(2,1)} fusion(bf16[32,128,512]{2,1,0:T(8,128)(2,1)} %get-tuple-element.123, s32[1024]{0:T(1024)S(1)} %pad_clamp_fusion.5), kind=kCustom, calls=%fused_computation.clone.clone.1 | custom fusion | bytes 8388736 | tf_op jit(solution)/shard_map/while/body/eval_jaxpr/jit(_take)/gather | solution.py:20
  73.5 7.2 %fusion.50 = f32[1,512,512]{2,1,0:T(8,128)S(1)} fusion(bf16[32,128,512]{2,1,0:T(8,128)(2,1)} %gather_fusion, pred[32]{0:T(512)(128)(4,1)S(1)} %get-tuple-element.101, bf16[32,128,512]{2,1,0:T(8,128)(2,1)} %gather_fusion.1, pred[32]{0:T(512)(128)(4,1)S(1)} %get-tuple-element.103, bf16[6,32,128,128]{3,2,1,0:T(8,128)(2,1)} %get-tuple-element.124, ...), kind=kOutput, calls=%fused_computation.10.clone.1 | convolution fusion | flops 2690646016 | bytes 10485828 | tf_op jit(solution)/shard_map/while/body/eval_jaxpr/dot_general | solution.py:21
  80.7 1.1 copy.34
  81.8 21.7 %dynamic_update_slice.5 = f32[6,512,512]{2,0,1:T(8,128)} dynamic-update-slice(f32[6,512,512]{2,0,1:T(8,128)} %get-tuple-element.113, f32[1,512,512]{2,0,1:T(1,128)S(1)} %copy.34, s32[]{:T(128)S(6)} %copy.38, s32[]{:T(128)} %constant.36.clone.1..sunk, s32[]{:T(128)} %constant.36.clone.1..sunk) | dynamic-update-slice | bytes 2097156 | tf_op jit(solution)/shard_map/while/body/jit(dynamic_update_index_in_dim)/dynamic_update_slice | solution.py:28
  103.6 0.7 compare_and_fusion.3
  104.3 5.0 %gather_fusion = bf16[32,128,512]{2,1,0:T(8,128)(2,1)} fusion(bf16[32,128,512]{2,1,0:T(8,128)(2,1)} %get-tuple-element.123, s32[1024]{0:T(1024)S(1)} %pad_clamp_fusion.4), kind=kCustom, calls=%fused_computation.1.clone.clone.1 | custom fusion | bytes 8388736 | tf_op jit(solution)/shard_map/while/body/eval_jaxpr/jit(_take)/gather | solution.py:17
  109.3 4.9 %gather_fusion.1 = bf16[32,128,512]{2,1,0:T(8,128)(2,1)} fusion(bf16[32,128,512]{2,1,0:T(8,128)(2,1)} %get-tuple-element.123, s32[1024]{0:T(1024)S(1)} %pad_clamp_fusion.5), kind=kCustom, calls=%fused_computation.clone.clone.1 | custom fusion | bytes 8388736 | tf_op jit(solution)/shard_map/while/body/eval_jaxpr/jit(_take)/gather | solution.py:20
  114.2 7.2 %fusion.50 = f32[1,512,512]{2,1,0:T(8,128)S(1)} fusion(bf16[32,128,512]{2,1,0:T(8,128)(2,1)} %gather_fusion, pred[32]{0:T(512)(128)(4,1)S(1)} %get-tuple-element.101, bf16[32,128,512]{2,1,0:T(8,128)(2,1)} %gather_fusion.1, pred[32]{0:T(512)(128)(4,1)S(1)} %get-tuple-element.103, bf16[6,32,128,128]{3,2,1,0:T(8,128)(2,1)} %get-tuple-element.124, ...), kind=kOutput, calls=%fused_computation.10.clone.1 | convolution fusion | flops 2690646016 | bytes 10485828 | tf_op jit(solution)/shard_map/while/body/eval_jaxpr/dot_general | solution.py:21
  121.5 1.1 copy.34
  122.6 21.7 %dynamic_update_slice.5 = f32[6,512,512]{2,0,1:T(8,128)} dynamic-update-slice(f32[6,512,512]{2,0,1:T(8,128)} %get-tuple-element.113, f32[1,512,512]{2,0,1:T(1,128)S(1)} %copy.34, s32[]{:T(128)S(6)} %copy.38, s32[]{:T(128)} %constant.36.clone.1..sunk, s32[]{:T(128)} %constant.36.clone.1..sunk) | dynamic-update-slice | bytes 2097156 | tf_op jit(solution)/shard_map/while/body/jit(dynamic_update_index_in_dim)/dynamic_update_slice | solution.py:28
  144.3 0.7 compare_and_fusion.3
  145.0 5.0 %gather_fusion = bf16[32,128,512]{2,1,0:T(8,128)(2,1)} fusion(bf16[32,128,512]{2,1,0:T(8,128)(2,1)} %get-tuple-element.123, s32[1024]{0:T(1024)S(1)} %pad_clamp_fusion.4), kind=kCustom, calls=%fused_computation.1.clone.clone.1 | custom fusion | bytes 8388736 | tf_op jit(solution)/shard_map/while/body/eval_jaxpr/jit(_take)/gather | solution.py:17
  150.1 4.9 %gather_fusion.1 = bf16[32,128,512]{2,1,0:T(8,128)(2,1)} fusion(bf16[32,128,512]{2,1,0:T(8,128)(2,1)} %get-tuple-element.123, s32[1024]{0:T(1024)S(1)} %pad_clamp_fusion.5), kind=kCustom, calls=%fused_computation.clone.clone.1 | custom fusion | bytes 8388736 | tf_op jit(solution)/shard_map/while/body/eval_jaxpr/jit(_take)/gather | solution.py:20
  155.0 7.2 %fusion.50 = f32[1,512,512]{2,1,0:T(8,128)S(1)} fusion(bf16[32,128,512]{2,1,0:T(8,128)(2,1)} %gather_fusion, pred[32]{0:T(512)(128)(4,1)S(1)} %get-tuple-element.101, bf16[32,128,512]{2,1,0:T(8,128)(2,1)} %gather_fusion.1, pred[32]{0:T(512)(128)(4,1)S(1)} %get-tuple-element.103, bf16[6,32,128,128]{3,2,1,0:T(8,128)(2,1)} %get-tuple-element.124, ...), kind=kOutput, calls=%fused_computation.10.clone.1 | convolution fusion | flops 2690646016 | bytes 10485828 | tf_op jit(solution)/shard_map/while/body/eval_jaxpr/dot_general | solution.py:21
  162.2 1.1 copy.34
  163.3 21.7 %dynamic_update_slice.5 = f32[6,512,512]{2,0,1:T(8,128)} dynamic-update-slice(f32[6,512,512]{2,0,1:T(8,128)} %get-tuple-element.113, f32[1,512,512]{2,0,1:T(1,128)S(1)} %copy.34, s32[]{:T(128)S(6)} %copy.38, s32[]{:T(128)} %constant.36.clone.1..sunk, s32[]{:T(128)} %constant.36.clone.1..sunk) | dynamic-update-slice | bytes 2097156 | tf_op jit(solution)/shard_map/while/body/jit(dynamic_update_index_in_dim)/dynamic_update_slice | solution.py:28
  185.1 0.7 compare_and_fusion.3
  185.8 5.0 %gather_fusion = bf16[32,128,512]{2,1,0:T(8,128)(2,1)} fusion(bf16[32,128,512]{2,1,0:T(8,128)(2,1)} %get-tuple-element.123, s32[1024]{0:T(1024)S(1)} %pad_clamp_fusion.4), kind=kCustom, calls=%fused_computation.1.clone.clone.1 | custom fusion | bytes 8388736 | tf_op jit(solution)/shard_map/while/body/eval_jaxpr/jit(_take)/gather | solution.py:17
  190.8 4.9 %gather_fusion.1 = bf16[32,128,512]{2,1,0:T(8,128)(2,1)} fusion(bf16[32,128,512]{2,1,0:T(8,128)(2,1)} %get-tuple-element.123, s32[1024]{0:T(1024)S(1)} %pad_clamp_fusion.5), kind=kCustom, calls=%fused_computation.clone.clone.1 | custom fusion | bytes 8388736 | tf_op jit(solution)/shard_map/while/body/eval_jaxpr/jit(_take)/gather | solution.py:20
  195.7 7.2 %fusion.50 = f32[1,512,512]{2,1,0:T(8,128)S(1)} fusion(bf16[32,128,512]{2,1,0:T(8,128)(2,1)} %gather_fusion, pred[32]{0:T(512)(128)(4,1)S(1)} %get-tuple-element.101, bf16[32,128,512]{2,1,0:T(8,128)(2,1)} %gather_fusion.1, pred[32]{0:T(512)(128)(4,1)S(1)} %get-tuple-element.103, bf16[6,32,128,128]{3,2,1,0:T(8,128)(2,1)} %get-tuple-element.124, ...), kind=kOutput, calls=%fused_computation.10.clone.1 | convolution fusion | flops 2690646016 | bytes 10485828 | tf_op jit(solution)/shard_map/while/body/eval_jaxpr/dot_general | solution.py:21
  203.0 1.1 copy.34
  204.1 21.7 %dynamic_update_slice.5 = f32[6,512,512]{2,0,1:T(8,128)} dynamic-update-slice(f32[6,512,512]{2,0,1:T(8,128)} %get-tuple-element.113, f32[1,512,512]{2,0,1:T(1,128)S(1)} %copy.34, s32[]{:T(128)S(6)} %copy.38, s32[]{:T(128)} %constant.36.clone.1..sunk, s32[]{:T(128)} %constant.36.clone.1..sunk) | dynamic-update-slice | bytes 2097156 | tf_op jit(solution)/shard_map/while/body/jit(dynamic_update_index_in_dim)/dynamic_update_slice | solution.py:28
  225.8 0.7 compare_and_fusion.3
  226.5 5.0 %gather_fusion = bf16[32,128,512]{2,1,0:T(8,128)(2,1)} fusion(bf16[32,128,512]{2,1,0:T(8,128)(2,1)} %get-tuple-element.123, s32[1024]{0:T(1024)S(1)} %pad_clamp_fusion.4), kind=kCustom, calls=%fused_computation.1.clone.clone.1 | custom fusion | bytes 8388736 | tf_op jit(solution)/shard_map/while/body/eval_jaxpr/jit(_take)/gather | solution.py:17
  231.6 4.9 %gather_fusion.1 = bf16[32,128,512]{2,1,0:T(8,128)(2,1)} fusion(bf16[32,128,512]{2,1,0:T(8,128)(2,1)} %get-tuple-element.123, s32[1024]{0:T(1024)S(1)} %pad_clamp_fusion.5), kind=kCustom, calls=%fused_computation.clone.clone.1 | custom fusion | bytes 8388736 | tf_op jit(solution)/shard_map/while/body/eval_jaxpr/jit(_take)/gather | solution.py:20
  236.5 7.2 %fusion.50 = f32[1,512,512]{2,1,0:T(8,128)S(1)} fusion(bf16[32,128,512]{2,1,0:T(8,128)(2,1)} %gather_fusion, pred[32]{0:T(512)(128)(4,1)S(1)} %get-tuple-element.101, bf16[32,128,512]{2,1,0:T(8,128)(2,1)} %gather_fusion.1, pred[32]{0:T(512)(128)(4,1)S(1)} %get-tuple-element.103, bf16[6,32,128,128]{3,2,1,0:T(8,128)(2,1)} %get-tuple-element.124, ...), kind=kOutput, calls=%fused_computation.10.clone.1 | convolution fusion | flops 2690646016 | bytes 10485828 | tf_op jit(solution)/shard_map/while/body/eval_jaxpr/dot_general | solution.py:21
  243.7 1.1 copy.34
  244.8 21.7 %dynamic_update_slice.5 = f32[6,512,512]{2,0,1:T(8,128)} dynamic-update-slice(f32[6,512,512]{2,0,1:T(8,128)} %get-tuple-element.113, f32[1,512,512]{2,0,1:T(1,128)S(1)} %copy.34, s32[]{:T(128)S(6)} %copy.38, s32[]{:T(128)} %constant.36.clone.1..sunk, s32[]{:T(128)} %constant.36.clone.1..sunk) | dynamic-update-slice | bytes 2097156 | tf_op jit(solution)/shard_map/while/body/jit(dynamic_update_index_in_dim)/dynamic_update_slice | solution.py:28
  266.6 0.7 compare_and_fusion.3
  267.3 5.0 %gather_fusion = bf16[32,128,512]{2,1,0:T(8,128)(2,1)} fusion(bf16[32,128,512]{2,1,0:T(8,128)(2,1)} %get-tuple-element.123, s32[1024]{0:T(1024)S(1)} %pad_clamp_fusion.4), kind=kCustom, calls=%fused_computation.1.clone.clone.1 | custom fusion | bytes 8388736 | tf_op jit(solution)/shard_map/while/body/eval_jaxpr/jit(_take)/gather | solution.py:17
  272.3 4.9 %gather_fusion.1 = bf16[32,128,512]{2,1,0:T(8,128)(2,1)} fusion(bf16[32,128,512]{2,1,0:T(8,128)(2,1)} %get-tuple-element.123, s32[1024]{0:T(1024)S(1)} %pad_clamp_fusion.5), kind=kCustom, calls=%fused_computation.clone.clone.1 | custom fusion | bytes 8388736 | tf_op jit(solution)/shard_map/while/body/eval_jaxpr/jit(_take)/gather | solution.py:20
  277.2 7.2 %fusion.50 = f32[1,512,512]{2,1,0:T(8,128)S(1)} fusion(bf16[32,128,512]{2,1,0:T(8,128)(2,1)} %gather_fusion, pred[32]{0:T(512)(128)(4,1)S(1)} %get-tuple-element.101, bf16[32,128,512]{2,1,0:T(8,128)(2,1)} %gather_fusion.1, pred[32]{0:T(512)(128)(4,1)S(1)} %get-tuple-element.103, bf16[6,32,128,128]{3,2,1,0:T(8,128)(2,1)} %get-tuple-element.124, ...), kind=kOutput, calls=%fused_computation.10.clone.1 | convolution fusion | flops 2690646016 | bytes 10485828 | tf_op jit(solution)/shard_map/while/body/eval_jaxpr/dot_general | solution.py:21
  284.5 1.1 copy.34
  285.6 21.7 %dynamic_update_slice.5 = f32[6,512,512]{2,0,1:T(8,128)} dynamic-update-slice(f32[6,512,512]{2,0,1:T(8,128)} %get-tuple-element.113, f32[1,512,512]{2,0,1:T(1,128)S(1)} %copy.34, s32[]{:T(128)S(6)} %copy.38, s32[]{:T(128)} %constant.36.clone.1..sunk, s32[]{:T(128)} %constant.36.clone.1..sunk) | dynamic-update-slice | bytes 2097156 | tf_op jit(solution)/shard_map/while/body/jit(dynamic_update_index_in_dim)/dynamic_update_slice | solution.py:28
  307.3 15.5 %reduce-scatter.2.cloned.1.call-done = f32[6,256,512]{2,0,1:T(8,128)} async-done(((f32[6,512,512]{2,0,1:T(8,128)}), f32[6,256,512]{2,0,1:T(8,128)}) %reduce-scatter.2.cloned.1.call-update) | async-done | bytes 3145744 | tf_op jit(solution)/shard_map/reduce_scatter | solution.py:29
  322.8 3.8 convert_element_type.39
  326.6 5.9 %all-to-all-start = ((bf16[6,256,512]{2,0,1:T(8,128)(2,1)}), bf16[6,256,512]{2,0,1:T(8,128)(2,1)S(1)}, u32[]{:S(2)}, u32[]{:S(2)}) async-start(bf16[6,256,512]{2,0,1:T(8,128)(2,1)} %convert_element_type.39), calls=%async_computation.1 | async-start | bytes 4194304 | tf_op jit(solution)/shard_map/all_to_all | solution.py:37
  332.6 48.5 %all-to-all-done = bf16[6,256,512]{2,0,1:T(8,128)(2,1)S(1)} async-done(((bf16[6,256,512]{2,0,1:T(8,128)(2,1)}), bf16[6,256,512]{2,0,1:T(8,128)(2,1)S(1)}, u32[]{:S(2)}, u32[]{:S(2)}) %all-to-all-start) | async-done | bytes 1572896 | tf_op jit(solution)/shard_map/all_to_all | solution.py:37
  381.6 2.9 convolution_convert_fusion
  384.5 1.8 copy.21
  386.2 74.3 %all_to_all.27 = bf16[2,48,32,512]{3,2,0,1:T(8,128)(2,1)S(1)} all-to-all(bf16[2,48,32,512]{3,2,0,1:T(8,128)(2,1)S(1)} %copy.21), channel_id=1, replica_groups=mesh['grp'=2,'blade'=8,'dof'=2] {'blade'}, dimensions={1} | all-to-all | bytes 6291456 | tf_op jit(solution)/shard_map/all_to_all | solution.py:41
  460.9 0.9 convert_bitcast_fusion
  461.9 3.4 copy.23
  (19 shorter events, 1.2 us)
Async XLA Ops:
  6.5 56.3 %all-gather.2.cloned.1.call-start = ((), (), s32[]{:S(2)}) async-start(), calls=%async_computation.3 | async-start | bytes 4456448 | tf_op jit(solution)/shard_map/all_gather | solution.py:12
  7.3 315.5 %reduce-scatter.2.cloned.1.call-start = ((), (), s32[]{:S(2)}) async-start(), calls=%async_computation.4 | async-start | bytes 12582912 | tf_op jit(solution)/shard_map/reduce_scatter | solution.py:29
  326.6 54.5 %all-to-all-start = ((bf16[6,256,512]{2,0,1:T(8,128)(2,1)}), bf16[6,256,512]{2,0,1:T(8,128)(2,1)S(1)}, u32[]{:S(2)}, u32[]{:S(2)}) async-start(bf16[6,256,512]{2,0,1:T(8,128)(2,1)} %convert_element_type.39), calls=%async_computation.1 | async-start | bytes 4194304 | tf_op jit(solution)/shard_map/all_to_all | solution.py:37
Sparse Core Ops, SparseCore 0:
  9.5 53.2 all-gather.1
  307.5 15.2 reduce-scatter.1

commit v2 on v1

--- a/solution.py
+++ b/solution.py
@@ -2,8 +2,521 @@
 
 import jax
 import jax.numpy as jnp
+import numpy as np
 from jax import lax
+from jax.experimental import pallas as pl
+from jax.experimental.pallas import tpu as pltpu
 from jax.sharding import PartitionSpec as P
+
+MESH = pl.DeviceIdType.MESH
+LAYERS = 4
+PAIR = 2
+BLOCK_GROUP = 8
+CHUNK = 32
+SUB = 16
+
+
+def dft_tables(per_chip):
+    per_layer = PAIR * per_chip
+    count = LAYERS * per_layer
+    index = np.arange(count)
+    angle = (index[:, None] * index[None, :] % count) * (2.0 * math.pi / count)
+    full = np.stack([np.cos(angle), -np.sin(angle)])
+
+    def rows_for(layer):
+        part = full[:, layer * per_layer : (layer + 1) * per_layer]
+        part = part.reshape(2, PAIR, per_chip, count).transpose(1, 0, 2, 3)
+        return part.reshape(2 * per_layer, count)
+
+    def split(weights):
+        wide = np.kron(weights, np.eye(SUB)).astype(np.float32)
+        high = wide.astype(jnp.bfloat16)
+        low = (wide - high.astype(np.float32)).astype(jnp.bfloat16)
+        return np.stack([high, low])
+
+    middle, ends = [], []
+    for layer, near in ((1, 0), (2, 3)):
+        partial = rows_for(near).copy()
+        partial[:, near * per_layer : (near + 1) * per_layer] = 0.0
+        middle.append(split(np.concatenate([rows_for(layer), partial])))
+        own = rows_for(near)[:, near * per_layer : (near + 1) * per_layer]
+        ends.append(split(own))
+    return np.stack(middle), np.stack(ends)
+
+
+def kernel(
+    panel_ref, stiff_hbm, rows_ref, cols_ref, wmid_hbm, wend_hbm, out_hbm,
+    pan, pan_t, stiff, acc, core_in, raw, y_out, wmid, wend,
+    comb_out, comb_in, harm_out, harm_in, out_v,
+    load_sem, up_send, up_recv, dn_send, dn_recv, ys_send, ys_recv, co_send, co_recv,
+    sum_send, sum_recv, sw_send, sw_recv, z_send, z_recv, h_send, h_recv, out_sem,
+):
+    blade = lax.axis_index("blade")
+    d = lax.axis_index("dof")
+    z = blade // PAIR
+    y = blade % PAIR
+    other_y = z * PAIR + (1 - y)
+    per_chip, n_blocks = stiff.shape[0], stiff.shape[1]
+    per_layer = per_chip * PAIR
+    rows_half = core_in.shape[1]
+    n_chunks = raw.shape[0]
+    half_cols = raw.shape[3]
+    per_shard = panel_ref.shape[0]
+
+    def to(src, dst, send, recv, **device):
+        return pltpu.make_async_remote_copy(
+            src_ref=src, dst_ref=dst, send_sem=send, recv_sem=recv,
+            device_id=device, device_id_type=MESH,
+        )
+
+    core = dict(dof=1 - d)
+    across = dict(blade=other_y)
+    up = dict(blade=jnp.minimum(blade + PAIR, LAYERS * PAIR - 1))
+    down = dict(blade=jnp.maximum(blade - PAIR, 0))
+    has_up = z < LAYERS - 1
+    has_dn = z > 0
+    is_mid = jnp.logical_and(has_up, has_dn)
+    is_end = jnp.logical_not(is_mid)
+    which = z // 2
+
+    load = pltpu.make_async_copy(stiff_hbm, stiff, load_sem.at[0])
+    load.start()
+    load_mid = pltpu.make_async_copy(wmid_hbm.at[which], wmid, load_sem.at[1])
+    load_mid.start()
+    load_end = pltpu.make_async_copy(wend_hbm.at[which], wend, load_sem.at[2])
+    load_end.start()
+
+    barrier = pltpu.get_barrier_semaphore()
+    pl.semaphore_signal(barrier, inc=1, device_id=core, device_id_type=MESH)
+    pl.semaphore_signal(barrier, inc=1, device_id=across, device_id_type=MESH)
+
+    @pl.when(has_up)
+    def _():
+        pl.semaphore_signal(barrier, inc=1, device_id=up, device_id_type=MESH)
+
+    @pl.when(has_dn)
+    def _():
+        pl.semaphore_signal(barrier, inc=1, device_id=down, device_id_type=MESH)
+
+    pl.semaphore_wait(barrier, 2 + has_up.astype(jnp.int32) + has_dn.astype(jnp.int32))
+
+    def shard(zz, yy, dd):
+        start = ((zz * PAIR + yy) * 2 + dd) * per_shard
+        return pan.at[pl.ds(start, per_shard)]
+
+    def flip(zz, yy, dd):
+        start = ((zz * PAIR + yy) * 2 + dd) * per_shard
+        for i in range(per_shard):
+            pan_t[start + i] = pan[start + i].T
+
+    def up_copy(step):
+        s = shard(jnp.maximum(z - step, 0), y, d)
+        return to(s, s, up_send.at[step], up_recv.at[step], **up)
+
+    def dn_copy(step):
+        s = shard(jnp.minimum(z + step, LAYERS - 1), y, d)
+        return to(s, s, dn_send.at[step], dn_recv.at[step], **down)
+
+    def up_arrival(step):
+        s = shard(jnp.maximum(z - step, 0), y, d)
+        return to(s, s, up_send.at[step - 1], up_recv.at[step - 1], **up)
+
+    def dn_arrival(step):
+        s = shard(jnp.minimum(z + step, LAYERS - 1), y, d)
+        return to(s, s, dn_send.at[step - 1], dn_recv.at[step - 1], **down)
+
+    def y_copy(zz):
+        s = shard(zz, y, d)
+        return to(s, s, ys_send.at[zz], ys_recv.at[zz], **across)
+
+    def y_arrival(zz):
+        s = shard(zz, 1 - y, d)
+        return to(s, s, ys_send.at[zz], ys_recv.at[zz], **across)
+
+    def core_copy(zz, yy):
+        s = shard(zz, yy, d)
+        return to(s, s, co_send.at[zz * PAIR + yy], co_recv.at[zz * PAIR + yy], **core)
+
+    def core_arrival(zz, yy):
+        s = shard(zz, yy, 1 - d)
+        return to(s, s, co_send.at[zz * PAIR + yy], co_recv.at[zz * PAIR + yy], **core)
+
+    mine = ((z * PAIR + y) * 2 + d) * per_shard
+    pan[pl.ds(mine, per_shard)] = panel_ref[...]
+
+    @pl.when(has_up)
+    def _():
+        up_copy(0).start()
+
+    @pl.when(has_dn)
+    def _():
+        dn_copy(0).start()
+
+    y_copy(z).start()
+    core_copy(z, y).start()
+    flip(z, y, d)
+
+    def take_y(zz):
+        y_arrival(zz).wait_recv()
+        core_copy(zz, 1 - y).start()
+        flip(zz, 1 - y, d)
+
+    for step in range(1, LAYERS):
+
+        @pl.when(z >= step)
+        def _(step=step):
+            up_arrival(step).wait_recv()
+            if step < LAYERS - 1:
+
+                @pl.when(has_up)
+                def _():
+                    up_copy(step).start()
+
+            y_copy(z - step).start()
+            core_copy(z - step, y).start()
+
+        @pl.when(z + step < LAYERS)
+        def _(step=step):
+            dn_arrival(step).wait_recv()
+            if step < LAYERS - 1:
+
+                @pl.when(has_dn)
+                def _():
+                    dn_copy(step).start()
+
+            y_copy(z + step).start()
+            core_copy(z + step, y).start()
+
+        @pl.when(z >= step)
+        def _(step=step):
+            flip(z - step, y, d)
+
+        @pl.when(z + step < LAYERS)
+        def _(step=step):
+            flip(z + step, y, d)
+
+        if step == 1:
+            take_y(z)
+        else:
+
+            @pl.when(z >= step - 1)
+            def _(step=step):
+                take_y(z - (step - 1))
+
+            @pl.when(z + step - 1 < LAYERS)
+            def _(step=step):
+                take_y(z + (step - 1))
+
+    last = LAYERS - 1
+
+    @pl.when(z >= last)
+    def _():
+        take_y(z - last)
+
+    @pl.when(z + last < LAYERS)
+    def _():
+        take_y(z + last)
+
+    def take_core(i, carry):
+        core_arrival(i // PAIR, i % PAIR).wait_recv()
+        flip(i // PAIR, i % PAIR, 1 - d)
+        return carry
+
+    lax.fori_loop(0, LAYERS * PAIR, take_core, 0)
+    load.wait()
+
+    def sum_copy(b):
+        src = acc.at[b, pl.ds(pl.multiple_of((1 - d) * rows_half, rows_half), rows_half)]
+        return to(src, core_in.at[b], sum_send.at[b], sum_recv.at[b], **core)
+
+    def slot(yy, b):
+        return z * per_layer + yy * per_chip + b
+
+    def swap_copy(b):
+        return to(y_out.at[b], raw.at[:, slot(y, b)], sw_send.at[b], sw_recv.at[b], **across)
+
+    def swap_arrival(b):
+        return to(y_out.at[b], raw.at[:, slot(1 - y, b)], sw_send.at[b], sw_recv.at[b], **across)
+
+    own_rows = pl.ds(pl.multiple_of(d * rows_half, rows_half), rows_half)
+
+    def summed(b, yy):
+        cols = pl.ds(pl.multiple_of(yy * half_cols, half_cols), half_cols)
+        total = acc[b, own_rows, cols] + core_in[b, :, cols]
+        return total.astype(jnp.bfloat16).reshape(n_chunks, CHUNK, half_cols)
+
+    def finish(b):
+        sum_copy(b).wait_recv()
+        y_out[b] = summed(b, 1 - y)
+        swap_copy(b).start()
+        raw[:, slot(y, b)] = summed(b, y)
+
+    def one_blade(b, carry):
+        acc[b] = jnp.zeros(acc.shape[1:], jnp.float32)
+
+        def group(q, carry):
+            left, image = [], []
+            for i in range(BLOCK_GROUP):
+                n = q * BLOCK_GROUP + i
+                product = jnp.dot(
+                    stiff[b, n], pan[cols_ref[b, n]], preferred_element_type=jnp.float32
+                )
+                image.append(product.astype(jnp.bfloat16))
+                left.append(pan_t[rows_ref[b, n]])
+            acc[b] += jnp.dot(
+                jnp.concatenate(left, axis=1),
+                jnp.concatenate(image, axis=0),
+                preferred_element_type=jnp.float32,
+            )
+            return carry
+
+        lax.fori_loop(0, n_blocks // BLOCK_GROUP, group, 0)
+        sum_copy(b).start()
+
+        @pl.when(b > 0)
+        def _():
+            finish(b - 1)
+
+        return carry
+
+    lax.fori_loop(0, per_chip, one_blade, 0)
+    finish(per_chip - 1)
+    load_mid.wait()
+    load_end.wait()
+
+    def take_swap(b, carry):
+        swap_arrival(b).wait_recv()
+        return carry
+
+    lax.fori_loop(0, per_chip, take_swap, 0)
+
+    n_harm = 2 * per_chip
+    near = jnp.where(z < 2, 0, LAYERS - 1)
+    far = LAYERS - 1 - z
+    near_dev = dict(blade=near * PAIR + y)
+    far_dev = dict(blade=far * PAIR + y)
+    mid_dev = dict(blade=jnp.where(z < 2, 1, LAYERS - 2) * PAIR + y)
+
+    def planes(p, zz):
+        return raw.at[p, pl.ds(zz * per_layer, per_layer)]
+
+    def end_copy(p):
+        s = planes(p, near)
+        return to(s, s, z_send.at[0, p], z_recv.at[0, p], **mid_dev)
+
+    def own_copy(p):
+        s = planes(p, z)
+        return to(s, s, z_send.at[1, p], z_recv.at[1, p], **far_dev)
+
+    def own_arrival(p):
+        s = planes(p, far)
+        return to(s, s, z_send.at[1, p], z_recv.at[1, p], **far_dev)
+
+    def pass_copy(p):
+        s = planes(p, near)
+        return to(s, s, z_send.at[2, p], z_recv.at[2, p], **far_dev)
+
+    def pass_arrival(p):
+        s = planes(p, LAYERS - 1 - near)
+        return to(s, s, z_send.at[2, p], z_recv.at[2, p], **far_dev)
+
+    def comb_copy(p):
+        return to(comb_out.at[p], comb_in.at[p], z_send.at[3, p], z_recv.at[3, p], **near_dev)
+
+    def harm_copy(p):
+        return to(harm_out.at[p], harm_in.at[p], h_send.at[p], h_recv.at[p], **across)
+
+    def out_copy(p):
+        rows = pl.ds(pl.multiple_of(p * CHUNK, CHUNK), CHUNK)
+        return pltpu.make_async_copy(out_v.at[:, rows], out_hbm.at[:, rows], out_sem.at[p])
+
+    def transform(weights, x):
+        return jnp.dot(weights[0], x, preferred_element_type=jnp.float32) + jnp.dot(
+            weights[1], x, preferred_element_type=jnp.float32
+        )
+
+    def store_final(p, sub, final):
+        rows = pl.ds(pl.multiple_of(p * CHUNK + sub * SUB, SUB), SUB)
+        cols = pl.ds(pl.multiple_of(y * half_cols, half_cols), half_cols)
+        mine = jnp.where(y == 0, final[0], final[1])
+        theirs = jnp.where(y == 0, final[1], final[0])
+        out_v[:, rows, cols] = mine
+        harm_out[p, :, pl.ds(sub * SUB, SUB)] = theirs.astype(jnp.bfloat16)
+
+    def take_harm(p):
+        harm_copy(p).wait_recv()
+        rows = pl.ds(pl.multiple_of(p * CHUNK, CHUNK), CHUNK)
+        cols = pl.ds(pl.multiple_of((1 - y) * half_cols, half_cols), half_cols)
+        out_v[:, rows, cols] = harm_in[p].astype(jnp.float32)
+        out_copy(p).start()
+
+    @pl.when(is_mid)
+    def _():
+        own_copy(0).start()
+        own_copy(1).start()
+        end_copy(0).wait_recv()
+        pass_copy(0).start()
+
+        def step(p, carry):
+            @pl.when(p + 1 < n_chunks)
+            def _():
+                end_copy(p + 1).wait_recv()
+                pass_copy(p + 1).start()
+
+            own_arrival(p).wait_recv()
+            pass_arrival(p).wait_recv()
+
+            @pl.when(p + 2 < n_chunks)
+            def _():
+                own_copy(p + 2).start()
+
+            for sub in range(CHUNK // SUB):
+                x = raw[p, :, pl.ds(sub * SUB, SUB)]
+                x = x.reshape(x.shape[0] * SUB, half_cols)
+                got = transform(wmid, x).reshape(4, n_harm, SUB, half_cols)
+                comb_out[p, :, pl.ds(sub * SUB, SUB)] = (
+                    got[2:].reshape(2 * n_harm, SUB, half_cols).astype(jnp.bfloat16)
+                )
+                store_final(p, sub, got[:2])
+            comb_copy(p).start()
+            harm_copy(p).start()
+
+            @pl.when(p > 0)
+            def _():
+                take_harm(p - 1)
+
+            return carry
+
+        lax.fori_loop(0, n_chunks, step, 0)
+
+    @pl.when(is_end)
+    def _():
+        for p in range(3):
+            end_copy(p).start()
+
+        def step(p, carry):
+            @pl.when(p + 3 < n_chunks)
+            def _():
+                end_copy(p + 3).start()
+
+            comb_copy(p).wait_recv()
+            for sub in range(CHUNK // SUB):
+                x = raw[p, pl.ds(z * per_layer, per_layer), pl.ds(sub * SUB, SUB)]
+                x = x.reshape(per_layer * SUB, half_cols)
+                got = transform(wend, x).reshape(2 * n_harm, SUB, half_cols)
+                got = got + comb_in[p, :, pl.ds(sub * SUB, SUB)].astype(jnp.float32)
+                store_final(p, sub, got.reshape(2, n_harm, SUB, half_cols))
+            harm_copy(p).start()
+
+            @pl.when(p > 0)
+            def _():
+                take_harm(p - 1)
+
+            return carry
+
+        lax.fori_loop(0, n_chunks, step, 0)
+
+    take_harm(n_chunks - 1)
+
+    for step in range(LAYERS - 1):
+
+        @pl.when(jnp.logical_and(has_up, z >= step))
+        def _(step=step):
+            up_copy(step).wait_send()
+
+        @pl.when(jnp.logical_and(has_dn, z + step < LAYERS))
+        def _(step=step):
+            dn_copy(step).wait_send()
+
+    for zz in range(LAYERS):
+        y_copy(zz).wait_send()
+        for yy in range(PAIR):
+            core_copy(zz, yy).wait_send()
+
+    def drain_blade(b, carry):
+        sum_copy(b).wait_send()
+        swap_copy(b).wait_send()
+        return carry
+
+    lax.fori_loop(0, per_chip, drain_blade, 0)
+
+    def drain_chunk(p, carry):
+        @pl.when(is_mid)
+        def _():
+            own_copy(p).wait_send()
+            pass_copy(p).wait_send()
+            comb_copy(p).wait_send()
+
+        @pl.when(is_end)
+        def _():
+            end_copy(p).wait_send()
+
+        harm_copy(p).wait_send()
+        out_copy(p).wait()
+        return carry
+
+    lax.fori_loop(0, n_chunks, drain_chunk, 0)
+
+
+def line_body(panel, stiffness, block_rows, block_cols):
+    per_chip, n_blocks, bs, _ = stiffness.shape
+    modes = panel.shape[-1]
+    shards = LAYERS * PAIR * 2
+    per_shard = panel.shape[0] // bs
+    n_all = shards * per_shard
+    half = modes // 2
+    n_chunks = half // CHUNK
+    count = LAYERS * PAIR * per_chip
+    n_harm = 2 * per_chip
+    wmid, wend = dft_tables(per_chip)
+    bf16, f32 = jnp.bfloat16, jnp.float32
+    dma = pltpu.SemaphoreType.DMA
+    vmem = pl.BlockSpec(memory_space=pltpu.VMEM)
+    smem = pl.BlockSpec(memory_space=pltpu.SMEM)
+    hbm = pl.BlockSpec(memory_space=pl.ANY)
+    result = pl.pallas_call(
+        kernel,
+        out_shape=jax.ShapeDtypeStruct((n_harm, half, modes), f32),
+        in_specs=[vmem, hbm, smem, smem, hbm, hbm],
+        out_specs=hbm,
+        scratch_shapes=[
+            pltpu.VMEM((n_all, bs, modes), bf16),
+            pltpu.VMEM((n_all, modes, bs), bf16),
+            pltpu.VMEM(stiffness.shape, bf16),
+            pltpu.VMEM((per_chip, modes, modes), f32),
+            pltpu.VMEM((per_chip, half, modes), f32),
+            pltpu.VMEM((n_chunks, count, CHUNK, half), bf16),
+            pltpu.VMEM((per_chip, n_chunks, CHUNK, half), bf16),
+            pltpu.VMEM(wmid.shape[1:], bf16),
+            pltpu.VMEM(wend.shape[1:], bf16),
+            pltpu.VMEM((n_chunks, 2 * n_harm, CHUNK, half), bf16),
+            pltpu.VMEM((n_chunks, 2 * n_harm, CHUNK, half), bf16),
+            pltpu.VMEM((n_chunks, n_harm, CHUNK, half), bf16),
+            pltpu.VMEM((n_chunks, n_harm, CHUNK, half), bf16),
+            pltpu.VMEM((n_harm, half, modes), f32),
+            dma((3,)),
+            dma((LAYERS - 1,)), dma((LAYERS - 1,)),
+            dma((LAYERS - 1,)), dma((LAYERS - 1,)),
+            dma((LAYERS,)), dma((LAYERS,)),
+            dma((LAYERS * PAIR,)), dma((LAYERS * PAIR,)),
+            dma((per_chip,)), dma((per_chip,)),
+            dma((per_chip,)), dma((per_chip,)),
+            dma((4, n_chunks)), dma((4, n_chunks)),
+            dma((n_chunks,)), dma((n_chunks,)),
+            dma((n_chunks,)),
+        ],
+        compiler_params=pltpu.CompilerParams(
+            collective_id=0, has_side_effects=True, vmem_limit_bytes=60 * 1024 * 1024
+        ),
+    )(
+        panel.reshape(per_shard, bs, modes),
+        stiffness,
+        block_rows,
+        block_cols,
+        jnp.asarray(wmid),
+        jnp.asarray(wend),
+    )
+    return result.reshape(2, per_chip, half, modes)
 
 
 def body(panel, stiffness, block_rows, block_cols):
@@ -49,8 +562,9 @@
         P(("grp", "blade"), "dof"),
         P(("grp", "blade"), "dof"),
     )
+    chips = mesh.shape["blade"]
     return jax.shard_map(
-        body,
+        line_body if chips == LAYERS * PAIR else body,
         mesh=mesh,
         in_specs=placed,
         out_specs=P(None, ("grp", "blade"), "dof", None),

time: 476 us -> 162 us (0.34)
  local copies, waits for them, and re-layouts: 203 us -> 6.2 us
  Pallas kernels: 0 us -> 155 us
  waiting for transfers between devices: 120 us -> 0 us
  blocking collectives: 74.3 us -> 0 us
  matrix products: 46.3 us -> 0 us
  between operations: 13.4 us -> 0.01 us
  other arithmetic: 9.17 us -> 0 us
  starting transfers between devices: 5.9 us -> 0 us
    pallas_call x0 -> x1, Pallas kernels: none -> 155 us  [line_body(): pl.pallas_call(kernel, out_shape=jax.ShapeDtypeStruct((n_harm, half, mode...]
    dynamic_update_slice x12 -> x0, local copies, waits for them, and re-layouts: 137 us -> none  [body(): partial_proj = lax.map(one_blade, (stiffness, block_rows, block_cols))]
    all_to_all x1 -> x0, blocking collectives: 74.3 us -> none  [body(): lax.all_to_all(joined, 'blade', split_axis=1, concat_axis=2, tiled=True)]
    gather x12 -> x0, local copies, waits for them, and re-layouts: 59.7 us -> none  [the longest x6 30.1 us: one_blade(): chosen = jnp.take(blocks, cols, axis=0)]
    all_gather x1 -> x0, waiting for transfers between devices: 55.5 us -> none  [body(): whole = lax.all_gather(panel, ('blade', 'dof'), axis=0, tiled=True)]
    all_to_all x1 -> x0, waiting for transfers between devices: 48.5 us -> none  [body(): lax.all_to_all(half, 'blade', split_axis=1, concat_axis=0, tiled=True)]
    dot_general x7 -> x0, matrix products: 46.3 us -> none  [the longest x6 43.5 us: one_blade(): lax.dot_general(left, image.reshape(-1, modes), (((0,), (0,)), ((), ())),...]
    reduce_scatter x1 -> x0, waiting for transfers between devices: 15.5 us -> none  [body(): lax.psum_scatter(partial_proj, 'dof', scatter_dimension=1, tiled=True)]
  transfers between devices with their start and end apart: 3 -> 0, of which waited for: 3 -> 0; matrix products, arithmetic and copies ran while one was open for 0% -> 0% of each run, Pallas kernels for 0% -> 0%
where the time goes in v2:
time: 162 us; the launch traced here: 161 us
  Pallas kernels  155 us (96%)
  local copies, waits for them, and re-layouts  6.2 us (4%)
    pallas_call x1, Pallas kernels, line_body(): pl.pallas_call(kernel, out_shape=jax.ShapeDtypeStruct((n_harm, half, mode...  155 us
    unnamed x1, local copies, waits for them, and re-layouts  6.2 us

profile of v2, /device:TPU:0, one launch (start us, length us, event | category | flops | bytes accessed | tf_op | source)
XLA Modules:
  0.0 161.5 jit_solution(9557743812832247262)
XLA Ops:
  0.0 155.3 %shard_map.64 = f32[12,256,512]{2,1,0:T(8,128)} custom-call(bf16[2,128,512]{2,1,0:T(8,128)(2,1)} %bitcast.3, bf16[6,32,128,128]{3,2,1,0:T(8,128)(2,1)} %stiff_hbm.1, s32[6,32]{1,0:T(8,128)} %rows_ref.1, s32[6,32]{1,0:T(8,128)} %cols_ref.1, bf16[2,2,768,768]{3,2,1,0:T(8,128)(2,1)} %constant.4.clone.wmid_hbm, bf16[2,2,384,192]{3,2,1,0:T(8,128)(2,1)} %constant.5.clone.wend_hbm), custom_call_target="tpu_custom_call" | custom-call | tf_op jit(solution)/shard_map/pallas_call | solution.py:477
  155.3 6.2 %copy.8 = f32[2,6,256,512]{3,2,1,0:T(8,128)} copy(f32[2,6,256,512]{3,2,1,0:T(8,128)} %bitcast.2) | data formatting | bytes 12582912

commit v3 on v2

--- a/solution.py
+++ b/solution.py
@@ -14,6 +14,8 @@
 BLOCK_GROUP = 8
 CHUNK = 32
 SUB = 16
+VMEM_BYTES = 60 * 1024 * 1024
+PASSES = 2
 
 
 def dft_tables(per_chip):
@@ -58,9 +60,11 @@
     other_y = z * PAIR + (1 - y)
     per_chip, n_blocks = stiff.shape[0], stiff.shape[1]
     per_layer = per_chip * PAIR
-    rows_half = core_in.shape[1]
+    rows_half = core_in.shape[2]
     n_chunks = raw.shape[0]
-    half_cols = raw.shape[3]
+    per_pass = n_chunks // PASSES
+    width = raw.shape[3]
+    half_cols = width * PASSES
     per_shard = panel_ref.shape[0]
 
     def to(src, dst, send, recv, **device):
@@ -161,6 +165,23 @@
         core_copy(zz, 1 - y).start()
         flip(zz, 1 - y, d)
 
+    def take_core(zz, yy):
+        core_arrival(zz, yy).wait_recv()
+        flip(zz, yy, 1 - d)
+
+    def at_distance(step, do):
+        if step == 0:
+            do(z)
+            return
+
+        @pl.when(z >= step)
+        def _():
+            do(z - step)
+
+        @pl.when(z + step < LAYERS)
+        def _():
+            do(z + step)
+
     for step in range(1, LAYERS):
 
         @pl.when(z >= step)
@@ -187,83 +208,62 @@
             y_copy(z + step).start()
             core_copy(z + step, y).start()
 
-        @pl.when(z >= step)
-        def _(step=step):
-            flip(z - step, y, d)
-
-        @pl.when(z + step < LAYERS)
-        def _(step=step):
-            flip(z + step, y, d)
-
-        if step == 1:
-            take_y(z)
-        else:
-
-            @pl.when(z >= step - 1)
-            def _(step=step):
-                take_y(z - (step - 1))
-
-            @pl.when(z + step - 1 < LAYERS)
-            def _(step=step):
-                take_y(z + (step - 1))
-
-    last = LAYERS - 1
-
-    @pl.when(z >= last)
-    def _():
-        take_y(z - last)
-
-    @pl.when(z + last < LAYERS)
-    def _():
-        take_y(z + last)
-
-    def take_core(i, carry):
-        core_arrival(i // PAIR, i % PAIR).wait_recv()
-        flip(i // PAIR, i % PAIR, 1 - d)
-        return carry
-
-    lax.fori_loop(0, LAYERS * PAIR, take_core, 0)
+        at_distance(step, lambda zz: flip(zz, y, d))
+        at_distance(step - 1, take_y)
+        at_distance(step - 1, lambda zz: take_core(zz, y))
+        if step > 1:
+            at_distance(step - 2, lambda zz: take_core(zz, 1 - y))
+
+    at_distance(LAYERS - 1, take_y)
+    at_distance(LAYERS - 1, lambda zz: take_core(zz, y))
+    at_distance(LAYERS - 2, lambda zz: take_core(zz, 1 - y))
+    at_distance(LAYERS - 1, lambda zz: take_core(zz, 1 - y))
     load.wait()
 
-    def sum_copy(b):
-        src = acc.at[b, pl.ds(pl.multiple_of((1 - d) * rows_half, rows_half), rows_half)]
-        return to(src, core_in.at[b], sum_send.at[b], sum_recv.at[b], **core)
+    def sum_copy(h, b):
+        src = acc.at[h, b, pl.ds(pl.multiple_of((1 - d) * rows_half, rows_half), rows_half)]
+        return to(src, core_in.at[h, b], sum_send.at[h, b], sum_recv.at[h, b], **core)
 
     def slot(yy, b):
         return z * per_layer + yy * per_chip + b
 
-    def swap_copy(b):
-        return to(y_out.at[b], raw.at[:, slot(y, b)], sw_send.at[b], sw_recv.at[b], **across)
-
-    def swap_arrival(b):
-        return to(y_out.at[b], raw.at[:, slot(1 - y, b)], sw_send.at[b], sw_recv.at[b], **across)
+    def swap_copy(h, b):
+        dst = raw.at[pl.ds(h * per_pass, per_pass), slot(y, b)]
+        return to(y_out.at[h, b], dst, sw_send.at[h, b], sw_recv.at[h, b], **across)
+
+    def swap_arrival(h, b):
+        dst = raw.at[pl.ds(h * per_pass, per_pass), slot(1 - y, b)]
+        return to(y_out.at[h, b], dst, sw_send.at[h, b], sw_recv.at[h, b], **across)
 
     own_rows = pl.ds(pl.multiple_of(d * rows_half, rows_half), rows_half)
 
-    def summed(b, yy):
-        cols = pl.ds(pl.multiple_of(yy * half_cols, half_cols), half_cols)
-        total = acc[b, own_rows, cols] + core_in[b, :, cols]
-        return total.astype(jnp.bfloat16).reshape(n_chunks, CHUNK, half_cols)
-
-    def finish(b):
-        sum_copy(b).wait_recv()
-        y_out[b] = summed(b, 1 - y)
-        swap_copy(b).start()
-        raw[:, slot(y, b)] = summed(b, y)
-
-    def one_blade(b, carry):
-        acc[b] = jnp.zeros(acc.shape[1:], jnp.float32)
+    def summed(h, b, yy):
+        cols = pl.ds(pl.multiple_of(yy * width, width), width)
+        total = acc[h, b, own_rows, cols] + core_in[h, b, :, cols]
+        return total.astype(jnp.bfloat16).reshape(per_pass, CHUNK, width)
+
+    def finish(h, b):
+        sum_copy(h, b).wait_recv()
+        y_out[h, b] = summed(h, b, 1 - y)
+        swap_copy(h, b).start()
+        raw[pl.ds(h * per_pass, per_pass), slot(y, b)] = summed(h, b, y)
+
+    def one_blade(h, b):
+        acc[h, b] = jnp.zeros(acc.shape[2:], jnp.float32)
 
         def group(q, carry):
             left, image = [], []
             for i in range(BLOCK_GROUP):
                 n = q * BLOCK_GROUP + i
-                product = jnp.dot(
-                    stiff[b, n], pan[cols_ref[b, n]], preferred_element_type=jnp.float32
+                c = cols_ref[b, n]
+                right = jnp.concatenate(
+                    [pan[c, :, pl.ds(yy * half_cols + h * width, width)] for yy in range(PAIR)],
+                    axis=1,
                 )
+                product = jnp.dot(stiff[b, n], right, preferred_element_type=jnp.float32)
                 image.append(product.astype(jnp.bfloat16))
                 left.append(pan_t[rows_ref[b, n]])
-            acc[b] += jnp.dot(
+            acc[h, b] += jnp.dot(
                 jnp.concatenate(left, axis=1),
                 jnp.concatenate(image, axis=0),
                 preferred_element_type=jnp.float32,
@@ -271,24 +271,27 @@
             return carry
 
         lax.fori_loop(0, n_blocks // BLOCK_GROUP, group, 0)
-        sum_copy(b).start()
+        sum_copy(h, b).start()
 
         @pl.when(b > 0)
         def _():
-            finish(b - 1)
-
+            finish(h, b - 1)
+
+    def end_pass(h):
+        finish(h, per_chip - 1)
+
+        def take_swap(b, carry):
+            swap_arrival(h, b).wait_recv()
+            return carry
+
+        lax.fori_loop(0, per_chip, take_swap, 0)
+
+    def first_pass(b, carry):
+        one_blade(0, b)
         return carry
 
-    lax.fori_loop(0, per_chip, one_blade, 0)
-    finish(per_chip - 1)
-    load_mid.wait()
-    load_end.wait()
-
-    def take_swap(b, carry):
-        swap_arrival(b).wait_recv()
-        return carry
-
-    lax.fori_loop(0, per_chip, take_swap, 0)
+    lax.fori_loop(0, per_chip, first_pass, 0)
+    end_pass(0)
 
     n_harm = 2 * per_chip
     near = jnp.where(z < 2, 0, LAYERS - 1)
@@ -326,29 +329,43 @@
     def harm_copy(p):
         return to(harm_out.at[p], harm_in.at[p], h_send.at[p], h_recv.at[p], **across)
 
-    def out_copy(p):
-        rows = pl.ds(pl.multiple_of(p * CHUNK, CHUNK), CHUNK)
-        return pltpu.make_async_copy(out_v.at[:, rows], out_hbm.at[:, rows], out_sem.at[p])
-
     def transform(weights, x):
-        return jnp.dot(weights[0], x, preferred_element_type=jnp.float32) + jnp.dot(
-            weights[1], x, preferred_element_type=jnp.float32
+        x = jnp.concatenate(
+            [x[:, i : i + SUB].reshape(-1, width) for i in range(0, CHUNK, SUB)], axis=1
         )
+        got = jnp.dot(weights[0], x, preferred_element_type=jnp.float32)
+        got = got + jnp.dot(weights[1], x, preferred_element_type=jnp.float32)
+        return [
+            got[:, i * width : (i + 1) * width].reshape(-1, SUB, width)
+            for i in range(CHUNK // SUB)
+        ]
+
+    def columns(p, yy):
+        return pl.ds(pl.multiple_of(yy * half_cols + p // per_pass * width, width), width)
+
+    def out_copy(r):
+        rows = pl.ds(pl.multiple_of(r * CHUNK, CHUNK), CHUNK)
+        return pltpu.make_async_copy(out_v.at[:, rows], out_hbm.at[:, rows], out_sem.at[r])
 
     def store_final(p, sub, final):
-        rows = pl.ds(pl.multiple_of(p * CHUNK + sub * SUB, SUB), SUB)
-        cols = pl.ds(pl.multiple_of(y * half_cols, half_cols), half_cols)
-        mine = jnp.where(y == 0, final[0], final[1])
-        theirs = jnp.where(y == 0, final[1], final[0])
-        out_v[:, rows, cols] = mine
+        row = lax.rem(p, per_pass) * CHUNK + sub * SUB
+        first, second = final[:n_harm], final[n_harm:]
+        out_v[:, pl.ds(pl.multiple_of(row, SUB), SUB), columns(p, y)] = jnp.where(
+            y == 0, first, second
+        )
+        theirs = jnp.where(y == 0, second, first)
         harm_out[p, :, pl.ds(sub * SUB, SUB)] = theirs.astype(jnp.bfloat16)
 
     def take_harm(p):
         harm_copy(p).wait_recv()
-        rows = pl.ds(pl.multiple_of(p * CHUNK, CHUNK), CHUNK)
-        cols = pl.ds(pl.multiple_of((1 - y) * half_cols, half_cols), half_cols)
-        out_v[:, rows, cols] = harm_in[p].astype(jnp.float32)
-        out_copy(p).start()
+        row = lax.rem(p, per_pass) * CHUNK
+        out_v[:, pl.ds(pl.multiple_of(row, CHUNK), CHUNK), columns(p, 1 - y)] = harm_in[
+            p
+        ].astype(jnp.float32)
+
+        @pl.when(p >= n_chunks - per_pass)
+        def _():
+            out_copy(p - (n_chunks - per_pass)).start()
 
     @pl.when(is_mid)
     def _():
@@ -357,7 +374,29 @@
         end_copy(0).wait_recv()
         pass_copy(0).start()
 
-        def step(p, carry):
+    @pl.when(is_end)
+    def _():
+        end_copy(0).start()
+        end_copy(1).start()
+
+    load_mid.wait()
+    load_end.wait()
+
+    def step(p, carry):
+        @pl.when(p < per_chip)
+        def _():
+            one_blade(1, p)
+
+        @pl.when(p == per_chip)
+        def _():
+            end_pass(1)
+
+        @pl.when(is_mid)
+        def _():
+            @pl.when(p + 2 < n_chunks)
+            def _():
+                own_copy(p + 2).start()
+
             @pl.when(p + 1 < n_chunks)
             def _():
                 end_copy(p + 1).wait_recv()
@@ -365,57 +404,32 @@
 
             own_arrival(p).wait_recv()
             pass_arrival(p).wait_recv()
-
+            for sub, got in enumerate(transform(wmid, raw[p])):
+                comb_out[p, :, pl.ds(sub * SUB, SUB)] = got[2 * n_harm :].astype(jnp.bfloat16)
+                store_final(p, sub, got[: 2 * n_harm])
+            comb_copy(p).start()
+
+        @pl.when(is_end)
+        def _():
             @pl.when(p + 2 < n_chunks)
             def _():
-                own_copy(p + 2).start()
-
-            for sub in range(CHUNK // SUB):
-                x = raw[p, :, pl.ds(sub * SUB, SUB)]
-                x = x.reshape(x.shape[0] * SUB, half_cols)
-                got = transform(wmid, x).reshape(4, n_harm, SUB, half_cols)
-                comb_out[p, :, pl.ds(sub * SUB, SUB)] = (
-                    got[2:].reshape(2 * n_harm, SUB, half_cols).astype(jnp.bfloat16)
-                )
-                store_final(p, sub, got[:2])
-            comb_copy(p).start()
-            harm_copy(p).start()
-
-            @pl.when(p > 0)
-            def _():
-                take_harm(p - 1)
-
-            return carry
-
-        lax.fori_loop(0, n_chunks, step, 0)
-
-    @pl.when(is_end)
-    def _():
-        for p in range(3):
-            end_copy(p).start()
-
-        def step(p, carry):
-            @pl.when(p + 3 < n_chunks)
-            def _():
-                end_copy(p + 3).start()
+                end_copy(p + 2).start()
 
             comb_copy(p).wait_recv()
-            for sub in range(CHUNK // SUB):
-                x = raw[p, pl.ds(z * per_layer, per_layer), pl.ds(sub * SUB, SUB)]
-                x = x.reshape(per_layer * SUB, half_cols)
-                got = transform(wend, x).reshape(2 * n_harm, SUB, half_cols)
-                got = got + comb_in[p, :, pl.ds(sub * SUB, SUB)].astype(jnp.float32)
-                store_final(p, sub, got.reshape(2, n_harm, SUB, half_cols))
-            harm_copy(p).start()
-
-            @pl.when(p > 0)
-            def _():
-                take_harm(p - 1)
-
-            return carry
-
-        lax.fori_loop(0, n_chunks, step, 0)
-
+            own = raw[p, pl.ds(z * per_layer, per_layer)]
+            for sub, got in enumerate(transform(wend, own)):
+                rows = pl.ds(sub * SUB, SUB)
+                store_final(p, sub, got + comb_in[p, :, rows].astype(jnp.float32))
+
+        harm_copy(p).start()
+
+        @pl.when(p > 0)
+        def _():
+            take_harm(p - 1)
+
+        return carry
+
+    lax.fori_loop(0, n_chunks, step, 0)
     take_harm(n_chunks - 1)
 
     for step in range(LAYERS - 1):
@@ -434,8 +448,9 @@
             core_copy(zz, yy).wait_send()
 
     def drain_blade(b, carry):
-        sum_copy(b).wait_send()
-        swap_copy(b).wait_send()
+        for h in range(PASSES):
+            sum_copy(h, b).wait_send()
+            swap_copy(h, b).wait_send()
         return carry
 
     lax.fori_loop(0, per_chip, drain_blade, 0)
@@ -452,10 +467,15 @@
             end_copy(p).wait_send()
 
         harm_copy(p).wait_send()
-        out_copy(p).wait()
         return carry
 
     lax.fori_loop(0, n_chunks, drain_chunk, 0)
+
+    def drain_out(r, carry):
+        out_copy(r).wait()
+        return carry
+
+    lax.fori_loop(0, per_pass, drain_out, 0)
 
 
 def line_body(panel, stiffness, block_rows, block_cols):
@@ -465,7 +485,9 @@
     per_shard = panel.shape[0] // bs
     n_all = shards * per_shard
     half = modes // 2
-    n_chunks = half // CHUNK
+    width = half // PASSES
+    per_pass = half // CHUNK
+    n_chunks = per_pass * PASSES
     count = LAYERS * PAIR * per_chip
     n_harm = 2 * per_chip
     wmid, wend = dft_tables(per_chip)
@@ -483,30 +505,30 @@
             pltpu.VMEM((n_all, bs, modes), bf16),
             pltpu.VMEM((n_all, modes, bs), bf16),
             pltpu.VMEM(stiffness.shape, bf16),
-            pltpu.VMEM((per_chip, modes, modes), f32),
-            pltpu.VMEM((per_chip, half, modes), f32),
-            pltpu.VMEM((n_chunks, count, CHUNK, half), bf16),
-            pltpu.VMEM((per_chip, n_chunks, CHUNK, half), bf16),
+            pltpu.VMEM((PASSES, per_chip, modes, PAIR * width), f32),
+            pltpu.VMEM((PASSES, per_chip, half, PAIR * width), f32),
+            pltpu.VMEM((n_chunks, count, CHUNK, width), bf16),
+            pltpu.VMEM((PASSES, per_chip, per_pass, CHUNK, width), bf16),
             pltpu.VMEM(wmid.shape[1:], bf16),
             pltpu.VMEM(wend.shape[1:], bf16),
-            pltpu.VMEM((n_chunks, 2 * n_harm, CHUNK, half), bf16),
-            pltpu.VMEM((n_chunks, 2 * n_harm, CHUNK, half), bf16),
-            pltpu.VMEM((n_chunks, n_harm, CHUNK, half), bf16),
-            pltpu.VMEM((n_chunks, n_harm, CHUNK, half), bf16),
+            pltpu.VMEM((n_chunks, 2 * n_harm, CHUNK, width), bf16),
+            pltpu.VMEM((n_chunks, 2 * n_harm, CHUNK, width), bf16),
+            pltpu.VMEM((n_chunks, n_harm, CHUNK, width), bf16),
+            pltpu.VMEM((n_chunks, n_harm, CHUNK, width), bf16),
             pltpu.VMEM((n_harm, half, modes), f32),
             dma((3,)),
             dma((LAYERS - 1,)), dma((LAYERS - 1,)),
             dma((LAYERS - 1,)), dma((LAYERS - 1,)),
             dma((LAYERS,)), dma((LAYERS,)),
             dma((LAYERS * PAIR,)), dma((LAYERS * PAIR,)),
-            dma((per_chip,)), dma((per_chip,)),
-            dma((per_chip,)), dma((per_chip,)),
+            dma((PASSES, per_chip)), dma((PASSES, per_chip)),
+            dma((PASSES, per_chip)), dma((PASSES, per_chip)),
             dma((4, n_chunks)), dma((4, n_chunks)),
             dma((n_chunks,)), dma((n_chunks,)),
-            dma((n_chunks,)),
+            dma((per_pass,)),
         ],
         compiler_params=pltpu.CompilerParams(
-            collective_id=0, has_side_effects=True, vmem_limit_bytes=60 * 1024 * 1024
+            collective_id=0, has_side_effects=True, vmem_limit_bytes=VMEM_BYTES
         ),
     )(
         panel.reshape(per_shard, bs, modes),

time: 162 us -> 172 us (1.062)
  Pallas kernels: 155 us -> 166 us
    pallas_call x1, Pallas kernels: 155 us -> 166 us  [line_body(): pl.pallas_call(kernel, out_shape=jax.ShapeDtypeStruct((n_harm, half, mode...]
where the time goes in v3:
time: 172 us
  Pallas kernels  166 us (97%)
  local copies, waits for them, and re-layouts  6.2 us (4%)
    pallas_call x1, Pallas kernels, line_body(): pl.pallas_call(kernel, out_shape=jax.ShapeDtypeStruct((n_harm, half, mode...  166 us
    unnamed x1, local copies, waits for them, and re-layouts  6.2 us

profile of v3, /device:TPU:0, one launch (start us, length us, event | category | flops | bytes accessed | tf_op | source)
XLA Modules:
  0.0 171.9 jit_solution(11109634031257453514)
XLA Ops:
  0.0 165.7 %shard_map.64 = f32[12,256,512]{2,1,0:T(8,128)} custom-call(bf16[2,128,512]{2,1,0:T(8,128)(2,1)} %bitcast.3, bf16[6,32,128,128]{3,2,1,0:T(8,128)(2,1)} %stiff_hbm.1, s32[6,32]{1,0:T(8,128)} %rows_ref.1, s32[6,32]{1,0:T(8,128)} %cols_ref.1, bf16[2,2,768,768]{3,2,1,0:T(8,128)(2,1)} %constant.4.clone.wmid_hbm, bf16[2,2,384,192]{3,2,1,0:T(8,128)(2,1)} %constant.5.clone.wend_hbm), custom_call_target="tpu_custom_call" | custom-call | tf_op jit(solution)/shard_map/pallas_call | solution.py:499
  165.7 6.2 %copy.8 = f32[2,6,256,512]{3,2,1,0:T(8,128)} copy(f32[2,6,256,512]{3,2,1,0:T(8,128)} %bitcast.2) | data formatting | bytes 12582912

commit v4 on v3

--- a/solution.py
+++ b/solution.py
@@ -12,10 +12,10 @@
 LAYERS = 4
 PAIR = 2
 BLOCK_GROUP = 8
-CHUNK = 32
+CHUNK = 16
 SUB = 16
 VMEM_BYTES = 60 * 1024 * 1024
-PASSES = 2
+PASSES = 1
 
 
 def dft_tables(per_chip):
@@ -256,10 +256,13 @@
             for i in range(BLOCK_GROUP):
                 n = q * BLOCK_GROUP + i
                 c = cols_ref[b, n]
-                right = jnp.concatenate(
-                    [pan[c, :, pl.ds(yy * half_cols + h * width, width)] for yy in range(PAIR)],
-                    axis=1,
-                )
+                if PASSES == 1:
+                    right = pan[c]
+                else:
+                    right = jnp.concatenate(
+                        [pan[c, :, pl.ds(yy * half_cols + h * width, width)] for yy in range(PAIR)],
+                        axis=1,
+                    )
                 product = jnp.dot(stiff[b, n], right, preferred_element_type=jnp.float32)
                 image.append(product.astype(jnp.bfloat16))
                 left.append(pan_t[rows_ref[b, n]])
@@ -383,13 +386,15 @@
     load_end.wait()
 
     def step(p, carry):
-        @pl.when(p < per_chip)
-        def _():
-            one_blade(1, p)
-
-        @pl.when(p == per_chip)
-        def _():
-            end_pass(1)
+        if PASSES > 1:
+
+            @pl.when(p < per_chip)
+            def _():
+                one_blade(1, p)
+
+            @pl.when(p == per_chip)
+            def _():
+                end_pass(1)
 
         @pl.when(is_mid)
         def _():

time: 172 us -> 172 us (level)
  no operation moved by 1% of the time
where the time goes in v4:
time: 172 us
  Pallas kernels  165 us (96%)
  local copies, waits for them, and re-layouts  6.2 us (4%)
    pallas_call x1, Pallas kernels, line_body(): pl.pallas_call(kernel, out_shape=jax.ShapeDtypeStruct((n_harm, half, mode...  165 us
    unnamed x1, local copies, waits for them, and re-layouts  6.2 us

profile of v4, /device:TPU:0, one launch (start us, length us, event | category | flops | bytes accessed | tf_op | source)
XLA Modules:
  0.0 171.5 jit_solution(11280547339995248341)
XLA Ops:
  0.0 165.3 %shard_map.64 = f32[12,256,512]{2,1,0:T(8,128)} custom-call(bf16[2,128,512]{2,1,0:T(8,128)(2,1)} %bitcast.3, bf16[6,32,128,128]{3,2,1,0:T(8,128)(2,1)} %stiff_hbm.1, s32[6,32]{1,0:T(8,128)} %rows_ref.1, s32[6,32]{1,0:T(8,128)} %cols_ref.1, bf16[2,2,768,768]{3,2,1,0:T(8,128)(2,1)} %constant.4.clone.wmid_hbm, bf16[2,2,384,192]{3,2,1,0:T(8,128)(2,1)} %constant.5.clone.wend_hbm), custom_call_target="tpu_custom_call" | custom-call | tf_op jit(solution)/shard_map/pallas_call | solution.py:504
  165.3 6.2 %copy.8 = f32[2,6,256,512]{3,2,1,0:T(8,128)} copy(f32[2,6,256,512]{3,2,1,0:T(8,128)} %bitcast.2) | data formatting | bytes 12582912

commit v5 on v4

--- a/solution.py
+++ b/solution.py
@@ -13,6 +13,8 @@
 PAIR = 2
 BLOCK_GROUP = 8
 CHUNK = 16
+AHEAD = 5
+PASS_AHEAD = 3
 SUB = 16
 VMEM_BYTES = 60 * 1024 * 1024
 PASSES = 1
@@ -373,14 +375,16 @@
     @pl.when(is_mid)
     def _():
         own_copy(0).start()
-        own_copy(1).start()
-        end_copy(0).wait_recv()
-        pass_copy(0).start()
+        for p in range(1, AHEAD):
+            own_copy(p).start()
+            if p <= PASS_AHEAD:
+                end_copy(p - 1).wait_recv()
+                pass_copy(p - 1).start()
 
     @pl.when(is_end)
     def _():
-        end_copy(0).start()
-        end_copy(1).start()
+        for p in range(AHEAD):
+            end_copy(p).start()
 
     load_mid.wait()
     load_end.wait()
@@ -388,24 +392,28 @@
     def step(p, carry):
         if PASSES > 1:
 
-            @pl.when(p < per_chip)
+            @pl.when(p < per_chip // 2)
             def _():
-                one_blade(1, p)
-
-            @pl.when(p == per_chip)
+                def second_pass(b, carry):
+                    one_blade(1, 2 * p + b)
+                    return carry
+
+                lax.fori_loop(0, 2, second_pass, 0)
+
+            @pl.when(p == per_chip // 2)
             def _():
                 end_pass(1)
 
         @pl.when(is_mid)
         def _():
-            @pl.when(p + 2 < n_chunks)
+            @pl.when(p + AHEAD < n_chunks)
             def _():
-                own_copy(p + 2).start()
-
-            @pl.when(p + 1 < n_chunks)
+                own_copy(p + AHEAD).start()
+
+            @pl.when(p + PASS_AHEAD < n_chunks)
             def _():
-                end_copy(p + 1).wait_recv()
-                pass_copy(p + 1).start()
+                end_copy(p + PASS_AHEAD).wait_recv()
+                pass_copy(p + PASS_AHEAD).start()
 
             own_arrival(p).wait_recv()
             pass_arrival(p).wait_recv()
@@ -416,9 +424,9 @@
 
         @pl.when(is_end)
         def _():
-            @pl.when(p + 2 < n_chunks)
+            @pl.when(p + AHEAD < n_chunks)
             def _():
-                end_copy(p + 2).start()
+                end_copy(p + AHEAD).start()
 
             comb_copy(p).wait_recv()
             own = raw[p, pl.ds(z * per_layer, per_layer)]

time: 172 us -> 157 us (0.913)
  Pallas kernels: 165 us -> 151 us
    pallas_call x1, Pallas kernels: 165 us -> 151 us  [line_body(): pl.pallas_call(kernel, out_shape=jax.ShapeDtypeStruct((n_harm, half, mode...]
where the time goes in v5:
time: 157 us
  Pallas kernels  151 us (96%)
  local copies, waits for them, and re-layouts  6.2 us (4%)
    pallas_call x1, Pallas kernels, line_body(): pl.pallas_call(kernel, out_shape=jax.ShapeDtypeStruct((n_harm, half, mode...  151 us
    unnamed x1, local copies, waits for them, and re-layouts  6.2 us

profile of v5, /device:TPU:0, one launch (start us, length us, event | category | flops | bytes accessed | tf_op | source)
XLA Modules:
  0.0 157.1 jit_solution(13085068811125310755)
XLA Ops:
  0.0 150.9 %shard_map.64 = f32[12,256,512]{2,1,0:T(8,128)} custom-call(bf16[2,128,512]{2,1,0:T(8,128)(2,1)} %bitcast.3, bf16[6,32,128,128]{3,2,1,0:T(8,128)(2,1)} %stiff_hbm.1, s32[6,32]{1,0:T(8,128)} %rows_ref.1, s32[6,32]{1,0:T(8,128)} %cols_ref.1, bf16[2,2,768,768]{3,2,1,0:T(8,128)(2,1)} %constant.4.clone.wmid_hbm, bf16[2,2,384,192]{3,2,1,0:T(8,128)(2,1)} %constant.5.clone.wend_hbm), custom_call_target="tpu_custom_call" | custom-call | tf_op jit(solution)/shard_map/pallas_call | solution.py:512
  150.9 6.2 %copy.8 = f32[2,6,256,512]{3,2,1,0:T(8,128)} copy(f32[2,6,256,512]{3,2,1,0:T(8,128)} %bitcast.2) | data formatting | bytes 12582912

commit v6 on v5

--- a/solution.py
+++ b/solution.py
@@ -12,12 +12,12 @@
 LAYERS = 4
 PAIR = 2
 BLOCK_GROUP = 8
-CHUNK = 16
+CHUNK = 32
 AHEAD = 5
 PASS_AHEAD = 3
 SUB = 16
 VMEM_BYTES = 60 * 1024 * 1024
-PASSES = 1
+PASSES = 2
 
 
 def dft_tables(per_chip):

time: 157 us -> 155 us (0.987)
  Pallas kernels: 151 us -> 149 us
    pallas_call x1, Pallas kernels: 151 us -> 149 us  [line_body(): pl.pallas_call(kernel, out_shape=jax.ShapeDtypeStruct((n_harm, half, mode...]
where the time goes in v6:
time: 155 us
  Pallas kernels  149 us (96%)
  local copies, waits for them, and re-layouts  6.2 us (4%)
    pallas_call x1, Pallas kernels, line_body(): pl.pallas_call(kernel, out_shape=jax.ShapeDtypeStruct((n_harm, half, mode...  149 us
    unnamed x1, local copies, waits for them, and re-layouts  6.2 us

profile of v6, /device:TPU:0, one launch (start us, length us, event | category | flops | bytes accessed | tf_op | source)
XLA Modules:
  0.0 155.2 jit_solution(1886239260505960360)
XLA Ops:
  0.0 149.0 %shard_map.64 = f32[12,256,512]{2,1,0:T(8,128)} custom-call(bf16[2,128,512]{2,1,0:T(8,128)(2,1)} %bitcast.3, bf16[6,32,128,128]{3,2,1,0:T(8,128)(2,1)} %stiff_hbm.1, s32[6,32]{1,0:T(8,128)} %rows_ref.1, s32[6,32]{1,0:T(8,128)} %cols_ref.1, bf16[2,2,768,768]{3,2,1,0:T(8,128)(2,1)} %constant.4.clone.wmid_hbm, bf16[2,2,384,192]{3,2,1,0:T(8,128)(2,1)} %constant.5.clone.wend_hbm), custom_call_target="tpu_custom_call" | custom-call | tf_op jit(solution)/shard_map/pallas_call | solution.py:512
  149.0 6.2 %copy.8 = f32[2,6,256,512]{3,2,1,0:T(8,128)} copy(f32[2,6,256,512]{3,2,1,0:T(8,128)} %bitcast.2) | data formatting | bytes 12582912

commit v7 on v6

--- a/solution.py
+++ b/solution.py
@@ -11,7 +11,7 @@
 MESH = pl.DeviceIdType.MESH
 LAYERS = 4
 PAIR = 2
-BLOCK_GROUP = 8
+BLOCK_GROUP = 32
 CHUNK = 32
 AHEAD = 5
 PASS_AHEAD = 3
@@ -251,9 +251,7 @@
         raw[pl.ds(h * per_pass, per_pass), slot(y, b)] = summed(h, b, y)
 
     def one_blade(h, b):
-        acc[h, b] = jnp.zeros(acc.shape[2:], jnp.float32)
-
-        def group(q, carry):
+        def group(q):
             left, image = [], []
             for i in range(BLOCK_GROUP):
                 n = q * BLOCK_GROUP + i
@@ -268,14 +266,21 @@
                 product = jnp.dot(stiff[b, n], right, preferred_element_type=jnp.float32)
                 image.append(product.astype(jnp.bfloat16))
                 left.append(pan_t[rows_ref[b, n]])
-            acc[h, b] += jnp.dot(
+            return jnp.dot(
                 jnp.concatenate(left, axis=1),
                 jnp.concatenate(image, axis=0),
                 preferred_element_type=jnp.float32,
             )
-            return carry
-
-        lax.fori_loop(0, n_blocks // BLOCK_GROUP, group, 0)
+
+        acc[h, b] = group(0)
+        if n_blocks > BLOCK_GROUP:
+
+            def more(q, carry):
+                acc[h, b] += group(q)
+                return carry
+
+            lax.fori_loop(1, n_blocks // BLOCK_GROUP, more, 0)
+
         sum_copy(h, b).start()
 
         @pl.when(b > 0)

time: 155 us -> 148 us (0.955)
  Pallas kernels: 149 us -> 141 us
    pallas_call x1, Pallas kernels: 149 us -> 141 us  [line_body(): pl.pallas_call(kernel, out_shape=jax.ShapeDtypeStruct((n_harm, half, mode...]
where the time goes in v7:
time: 148 us; the launch traced here: 147 us
  Pallas kernels  141 us (95%)
  local copies, waits for them, and re-layouts  6.2 us (4%)
    pallas_call x1, Pallas kernels, line_body(): pl.pallas_call(kernel, out_shape=jax.ShapeDtypeStruct((n_harm, half, mode...  141 us
    unnamed x1, local copies, waits for them, and re-layouts  6.2 us

profile of v7, /device:TPU:0, one launch (start us, length us, event | category | flops | bytes accessed | tf_op | source)
XLA Modules:
  0.0 147.5 jit_solution(979329012730863868)
XLA Ops:
  0.0 141.3 %shard_map.64 = f32[12,256,512]{2,1,0:T(8,128)} custom-call(bf16[2,128,512]{2,1,0:T(8,128)(2,1)} %bitcast.3, bf16[6,32,128,128]{3,2,1,0:T(8,128)(2,1)} %stiff_hbm.1, s32[6,32]{1,0:T(8,128)} %rows_ref.1, s32[6,32]{1,0:T(8,128)} %cols_ref.1, bf16[2,2,768,768]{3,2,1,0:T(8,128)(2,1)} %constant.4.clone.wmid_hbm, bf16[2,2,384,192]{3,2,1,0:T(8,128)(2,1)} %constant.5.clone.wend_hbm), custom_call_target="tpu_custom_call" | custom-call | tf_op jit(solution)/shard_map/pallas_call | solution.py:517
  141.3 6.2 %copy.8 = f32[2,6,256,512]{3,2,1,0:T(8,128)} copy(f32[2,6,256,512]{3,2,1,0:T(8,128)} %bitcast.2) | data formatting | bytes 12582912

commit v8 on v7

--- a/solution.py
+++ b/solution.py
@@ -106,70 +106,75 @@
 
     pl.semaphore_wait(barrier, 2 + has_up.astype(jnp.int32) + has_dn.astype(jnp.int32))
 
-    def shard(zz, yy, dd):
-        start = ((zz * PAIR + yy) * 2 + dd) * per_shard
-        return pan.at[pl.ds(start, per_shard)]
-
-    def flip(zz, yy, dd):
-        start = ((zz * PAIR + yy) * 2 + dd) * per_shard
-        for i in range(per_shard):
-            pan_t[start + i] = pan[start + i].T
-
-    def up_copy(step):
-        s = shard(jnp.maximum(z - step, 0), y, d)
-        return to(s, s, up_send.at[step], up_recv.at[step], **up)
-
-    def dn_copy(step):
-        s = shard(jnp.minimum(z + step, LAYERS - 1), y, d)
-        return to(s, s, dn_send.at[step], dn_recv.at[step], **down)
-
-    def up_arrival(step):
-        s = shard(jnp.maximum(z - step, 0), y, d)
-        return to(s, s, up_send.at[step - 1], up_recv.at[step - 1], **up)
-
-    def dn_arrival(step):
-        s = shard(jnp.minimum(z + step, LAYERS - 1), y, d)
-        return to(s, s, dn_send.at[step - 1], dn_recv.at[step - 1], **down)
-
-    def y_copy(zz):
-        s = shard(zz, y, d)
-        return to(s, s, ys_send.at[zz], ys_recv.at[zz], **across)
-
-    def y_arrival(zz):
-        s = shard(zz, 1 - y, d)
-        return to(s, s, ys_send.at[zz], ys_recv.at[zz], **across)
-
-    def core_copy(zz, yy):
-        s = shard(zz, yy, d)
-        return to(s, s, co_send.at[zz * PAIR + yy], co_recv.at[zz * PAIR + yy], **core)
-
-    def core_arrival(zz, yy):
-        s = shard(zz, yy, 1 - d)
-        return to(s, s, co_send.at[zz * PAIR + yy], co_recv.at[zz * PAIR + yy], **core)
-
-    mine = ((z * PAIR + y) * 2 + d) * per_shard
-    pan[pl.ds(mine, per_shard)] = panel_ref[...]
-
-    @pl.when(has_up)
-    def _():
-        up_copy(0).start()
-
-    @pl.when(has_dn)
-    def _():
-        dn_copy(0).start()
-
-    y_copy(z).start()
-    core_copy(z, y).start()
-    flip(z, y, d)
-
-    def take_y(zz):
-        y_arrival(zz).wait_recv()
-        core_copy(zz, 1 - y).start()
-        flip(zz, 1 - y, d)
-
-    def take_core(zz, yy):
-        core_arrival(zz, yy).wait_recv()
-        flip(zz, yy, 1 - d)
+    def place(zz, yy, dd, k):
+        return ((zz * PAIR + yy) * 2 + dd) * per_shard + k
+
+    def shard(zz, yy, dd, k):
+        return pan.at[pl.ds(place(zz, yy, dd, k), 1)]
+
+    def flip(zz, yy, dd, k):
+        n = place(zz, yy, dd, k)
+        pan_t[n] = pan[n].T
+
+    def up_copy(step, k):
+        s = shard(jnp.maximum(z - step, 0), y, d, k)
+        return to(s, s, up_send.at[step, k], up_recv.at[step, k], **up)
+
+    def dn_copy(step, k):
+        s = shard(jnp.minimum(z + step, LAYERS - 1), y, d, k)
+        return to(s, s, dn_send.at[step, k], dn_recv.at[step, k], **down)
+
+    def up_arrival(step, k):
+        s = shard(jnp.maximum(z - step, 0), y, d, k)
+        return to(s, s, up_send.at[step - 1, k], up_recv.at[step - 1, k], **up)
+
+    def dn_arrival(step, k):
+        s = shard(jnp.minimum(z + step, LAYERS - 1), y, d, k)
+        return to(s, s, dn_send.at[step - 1, k], dn_recv.at[step - 1, k], **down)
+
+    def y_copy(zz, k):
+        s = shard(zz, y, d, k)
+        return to(s, s, ys_send.at[zz, k], ys_recv.at[zz, k], **across)
+
+    def y_arrival(zz, k):
+        s = shard(zz, 1 - y, d, k)
+        return to(s, s, ys_send.at[zz, k], ys_recv.at[zz, k], **across)
+
+    def core_copy(zz, yy, k):
+        s = shard(zz, yy, d, k)
+        i = zz * PAIR + yy
+        return to(s, s, co_send.at[i, k], co_recv.at[i, k], **core)
+
+    def core_arrival(zz, yy, k):
+        s = shard(zz, yy, 1 - d, k)
+        i = zz * PAIR + yy
+        return to(s, s, co_send.at[i, k], co_recv.at[i, k], **core)
+
+    for k in range(per_shard):
+        pan[place(z, y, d, k)] = panel_ref[k]
+
+        @pl.when(has_up)
+        def _(k=k):
+            up_copy(0, k).start()
+
+        @pl.when(has_dn)
+        def _(k=k):
+            dn_copy(0, k).start()
+
+        y_copy(z, k).start()
+        core_copy(z, y, k).start()
+
+    for k in range(per_shard):
+        flip(z, y, d, k)
+
+    def take_y(zz, k):
+        y_arrival(zz, k).wait_recv()
+        core_copy(zz, 1 - y, k).start()
+        flip(zz, 1 - y, d, k)
+
+    def take_core(zz, yy, k):
+        core_arrival(zz, yy, k).wait_recv()
+        flip(zz, yy, 1 - d, k)
 
     def at_distance(step, do):
         if step == 0:
@@ -185,41 +190,44 @@
             do(z + step)
 
     for step in range(1, LAYERS):
-
-        @pl.when(z >= step)
-        def _(step=step):
-            up_arrival(step).wait_recv()
-            if step < LAYERS - 1:
-
-                @pl.when(has_up)
-                def _():
-                    up_copy(step).start()
-
-            y_copy(z - step).start()
-            core_copy(z - step, y).start()
-
-        @pl.when(z + step < LAYERS)
-        def _(step=step):
-            dn_arrival(step).wait_recv()
-            if step < LAYERS - 1:
-
-                @pl.when(has_dn)
-                def _():
-                    dn_copy(step).start()
-
-            y_copy(z + step).start()
-            core_copy(z + step, y).start()
-
-        at_distance(step, lambda zz: flip(zz, y, d))
-        at_distance(step - 1, take_y)
-        at_distance(step - 1, lambda zz: take_core(zz, y))
-        if step > 1:
-            at_distance(step - 2, lambda zz: take_core(zz, 1 - y))
-
-    at_distance(LAYERS - 1, take_y)
-    at_distance(LAYERS - 1, lambda zz: take_core(zz, y))
-    at_distance(LAYERS - 2, lambda zz: take_core(zz, 1 - y))
-    at_distance(LAYERS - 1, lambda zz: take_core(zz, 1 - y))
+        for k in range(per_shard):
+
+            @pl.when(z >= step)
+            def _(step=step, k=k):
+                up_arrival(step, k).wait_recv()
+                if step < LAYERS - 1:
+
+                    @pl.when(has_up)
+                    def _():
+                        up_copy(step, k).start()
+
+                y_copy(z - step, k).start()
+                core_copy(z - step, y, k).start()
+
+            @pl.when(z + step < LAYERS)
+            def _(step=step, k=k):
+                dn_arrival(step, k).wait_recv()
+                if step < LAYERS - 1:
+
+                    @pl.when(has_dn)
+                    def _():
+                        dn_copy(step, k).start()
+
+                y_copy(z + step, k).start()
+                core_copy(z + step, y, k).start()
+
+            at_distance(step, lambda zz: flip(zz, y, d, k))
+            at_distance(step - 1, lambda zz: take_y(zz, k))
+            at_distance(step - 1, lambda zz: take_core(zz, y, k))
+            if step > 1:
+                at_distance(step - 2, lambda zz: take_core(zz, 1 - y, k))
+
+    for k in range(per_shard):
+        at_distance(LAYERS - 2, lambda zz: take_core(zz, 1 - y, k))
+        at_distance(LAYERS - 1, lambda zz: take_core(zz, y, k))
+        at_distance(LAYERS - 1, lambda zz: take_y(zz, k))
+    for k in range(per_shard):
+        at_distance(LAYERS - 1, lambda zz: take_core(zz, 1 - y, k))
     load.wait()
 
     def sum_copy(h, b):
@@ -450,20 +458,21 @@
     lax.fori_loop(0, n_chunks, step, 0)
     take_harm(n_chunks - 1)
 
-    for step in range(LAYERS - 1):
-
-        @pl.when(jnp.logical_and(has_up, z >= step))
-        def _(step=step):
-            up_copy(step).wait_send()
-
-        @pl.when(jnp.logical_and(has_dn, z + step < LAYERS))
-        def _(step=step):
-            dn_copy(step).wait_send()
-
-    for zz in range(LAYERS):
-        y_copy(zz).wait_send()
-        for yy in range(PAIR):
-            core_copy(zz, yy).wait_send()
+    for k in range(per_shard):
+        for step in range(LAYERS - 1):
+
+            @pl.when(jnp.logical_and(has_up, z >= step))
+            def _(step=step, k=k):
+                up_copy(step, k).wait_send()
+
+            @pl.when(jnp.logical_and(has_dn, z + step < LAYERS))
+            def _(step=step, k=k):
+                dn_copy(step, k).wait_send()
+
+        for zz in range(LAYERS):
+            y_copy(zz, k).wait_send()
+            for yy in range(PAIR):
+                core_copy(zz, yy, k).wait_send()
 
     def drain_blade(b, carry):
         for h in range(PASSES):
@@ -535,10 +544,10 @@
             pltpu.VMEM((n_chunks, n_harm, CHUNK, width), bf16),
             pltpu.VMEM((n_harm, half, modes), f32),
             dma((3,)),
-            dma((LAYERS - 1,)), dma((LAYERS - 1,)),
-            dma((LAYERS - 1,)), dma((LAYERS - 1,)),
-            dma((LAYERS,)), dma((LAYERS,)),
-            dma((LAYERS * PAIR,)), dma((LAYERS * PAIR,)),
+            dma((LAYERS - 1, per_shard)), dma((LAYERS - 1, per_shard)),
+            dma((LAYERS - 1, per_shard)), dma((LAYERS - 1, per_shard)),
+            dma((LAYERS, per_shard)), dma((LAYERS, per_shard)),
+            dma((LAYERS * PAIR, per_shard)), dma((LAYERS * PAIR, per_shard)),
             dma((PASSES, per_chip)), dma((PASSES, per_chip)),
             dma((PASSES, per_chip)), dma((PASSES, per_chip)),
             dma((4, n_chunks)), dma((4, n_chunks)),

time: 148 us -> 145 us (0.980)
  Pallas kernels: 141 us -> 138 us
    pallas_call x1, Pallas kernels: 141 us -> 138 us  [line_body(): pl.pallas_call(kernel, out_shape=jax.ShapeDtypeStruct((n_harm, half, mode...]
where the time goes in v8:
time: 145 us; the launch traced here: 144 us
  Pallas kernels  138 us (95%)
  local copies, waits for them, and re-layouts  6.2 us (4%)
    pallas_call x1, Pallas kernels, line_body(): pl.pallas_call(kernel, out_shape=jax.ShapeDtypeStruct((n_harm, half, mode...  138 us
    unnamed x1, local copies, waits for them, and re-layouts  6.2 us

profile of v8, /device:TPU:0, one launch (start us, length us, event | category | flops | bytes accessed | tf_op | source)
XLA Modules:
  0.0 144.4 jit_solution(12718990603165910227)
XLA Ops:
  0.0 138.2 %shard_map.64 = f32[12,256,512]{2,1,0:T(8,128)} custom-call(bf16[2,128,512]{2,1,0:T(8,128)(2,1)} %bitcast.3, bf16[6,32,128,128]{3,2,1,0:T(8,128)(2,1)} %stiff_hbm.1, s32[6,32]{1,0:T(8,128)} %rows_ref.1, s32[6,32]{1,0:T(8,128)} %cols_ref.1, bf16[2,2,768,768]{3,2,1,0:T(8,128)(2,1)} %constant.4.clone.wmid_hbm, bf16[2,2,384,192]{3,2,1,0:T(8,128)(2,1)} %constant.5.clone.wend_hbm), custom_call_target="tpu_custom_call" | custom-call | tf_op jit(solution)/shard_map/pallas_call | solution.py:526
  138.2 6.2 %copy.8 = f32[2,6,256,512]{3,2,1,0:T(8,128)} copy(f32[2,6,256,512]{3,2,1,0:T(8,128)} %bitcast.2) | data formatting | bytes 12582912

commit v9 on v8

--- a/solution.py
+++ b/solution.py
@@ -14,6 +14,7 @@
 BLOCK_GROUP = 32
 CHUNK = 32
 AHEAD = 5
+EARLY = 3
 PASS_AHEAD = 3
 SUB = 16
 VMEM_BYTES = 60 * 1024 * 1024
@@ -399,21 +400,25 @@
         for p in range(AHEAD):
             end_copy(p).start()
 
+    if PASSES > 1:
+
+        def second_pass(b, carry):
+            one_blade(1, b)
+            return carry
+
+        lax.fori_loop(0, EARLY, second_pass, 0)
+
     load_mid.wait()
     load_end.wait()
 
     def step(p, carry):
         if PASSES > 1:
 
-            @pl.when(p < per_chip // 2)
+            @pl.when(p < per_chip - EARLY)
             def _():
-                def second_pass(b, carry):
-                    one_blade(1, 2 * p + b)
-                    return carry
-
-                lax.fori_loop(0, 2, second_pass, 0)
-
-            @pl.when(p == per_chip // 2)
+                one_blade(1, p + EARLY)
+
+            @pl.when(p == per_chip - EARLY)
             def _():
                 end_pass(1)
 

time: 145 us -> 147 us (1.014)
  Pallas kernels: 138 us -> 140 us
    pallas_call x1, Pallas kernels: 138 us -> 140 us  [line_body(): pl.pallas_call(kernel, out_shape=jax.ShapeDtypeStruct((n_harm, half, mode...]
where the time goes in v9:
time: 147 us
  Pallas kernels  140 us (95%)
  local copies, waits for them, and re-layouts  6.2 us (4%)
    pallas_call x1, Pallas kernels, line_body(): pl.pallas_call(kernel, out_shape=jax.ShapeDtypeStruct((n_harm, half, mode...  140 us
    unnamed x1, local copies, waits for them, and re-layouts  6.2 us

profile of v9, /device:TPU:0, one launch (start us, length us, event | category | flops | bytes accessed | tf_op | source)
XLA Modules:
  0.0 146.5 jit_solution(16275456682956539366)
XLA Ops:
  0.0 140.3 %shard_map.64 = f32[12,256,512]{2,1,0:T(8,128)} custom-call(bf16[2,128,512]{2,1,0:T(8,128)(2,1)} %bitcast.3, bf16[6,32,128,128]{3,2,1,0:T(8,128)(2,1)} %stiff_hbm.1, s32[6,32]{1,0:T(8,128)} %rows_ref.1, s32[6,32]{1,0:T(8,128)} %cols_ref.1, bf16[2,2,768,768]{3,2,1,0:T(8,128)(2,1)} %constant.4.clone.wmid_hbm, bf16[2,2,384,192]{3,2,1,0:T(8,128)(2,1)} %constant.5.clone.wend_hbm), custom_call_target="tpu_custom_call" | custom-call | tf_op jit(solution)/shard_map/pallas_call | solution.py:531
  140.3 6.2 %copy.8 = f32[2,6,256,512]{3,2,1,0:T(8,128)} copy(f32[2,6,256,512]{3,2,1,0:T(8,128)} %bitcast.2) | data formatting | bytes 12582912

commit v10 on v8

--- a/solution.py
+++ b/solution.py
@@ -405,6 +405,29 @@
     def step(p, carry):
         if PASSES > 1:
 
+            @pl.when(p == per_chip // 2)
+            def _():
+                end_pass(1)
+
+        @pl.when(is_mid)
+        def _():
+            @pl.when(p + AHEAD < n_chunks)
+            def _():
+                own_copy(p + AHEAD).start()
+
+            @pl.when(p + PASS_AHEAD < n_chunks)
+            def _():
+                end_copy(p + PASS_AHEAD).wait_recv()
+                pass_copy(p + PASS_AHEAD).start()
+
+        @pl.when(is_end)
+        def _():
+            @pl.when(p + AHEAD < n_chunks)
+            def _():
+                end_copy(p + AHEAD).start()
+
+        if PASSES > 1:
+
             @pl.when(p < per_chip // 2)
             def _():
                 def second_pass(b, carry):
@@ -413,21 +436,8 @@
 
                 lax.fori_loop(0, 2, second_pass, 0)
 
-            @pl.when(p == per_chip // 2)
-            def _():
-                end_pass(1)
-
         @pl.when(is_mid)
         def _():
-            @pl.when(p + AHEAD < n_chunks)
-            def _():
-                own_copy(p + AHEAD).start()
-
-            @pl.when(p + PASS_AHEAD < n_chunks)
-            def _():
-                end_copy(p + PASS_AHEAD).wait_recv()
-                pass_copy(p + PASS_AHEAD).start()
-
             own_arrival(p).wait_recv()
             pass_arrival(p).wait_recv()
             for sub, got in enumerate(transform(wmid, raw[p])):
@@ -437,10 +447,6 @@
 
         @pl.when(is_end)
         def _():
-            @pl.when(p + AHEAD < n_chunks)
-            def _():
-                end_copy(p + AHEAD).start()
-
             comb_copy(p).wait_recv()
             own = raw[p, pl.ds(z * per_layer, per_layer)]
             for sub, got in enumerate(transform(wend, own)):

time: 145 us -> 147 us (1.014)
  Pallas kernels: 138 us -> 140 us
    pallas_call x1, Pallas kernels: 138 us -> 140 us  [line_body(): pl.pallas_call(kernel, out_shape=jax.ShapeDtypeStruct((n_harm, half, mode...]
where the time goes in v10:
time: 147 us; the launch traced here: 146 us
  Pallas kernels  140 us (95%)
  local copies, waits for them, and re-layouts  6.2 us (4%)
    pallas_call x1, Pallas kernels, line_body(): pl.pallas_call(kernel, out_shape=jax.ShapeDtypeStruct((n_harm, half, mode...  140 us
    unnamed x1, local copies, waits for them, and re-layouts  6.2 us

profile of v10, /device:TPU:0, one launch (start us, length us, event | category | flops | bytes accessed | tf_op | source)
XLA Modules:
  0.0 146.5 jit_solution(5560871369148880357)
XLA Ops:
  0.0 140.3 %shard_map.64 = f32[12,256,512]{2,1,0:T(8,128)} custom-call(bf16[2,128,512]{2,1,0:T(8,128)(2,1)} %bitcast.3, bf16[6,32,128,128]{3,2,1,0:T(8,128)(2,1)} %stiff_hbm.1, s32[6,32]{1,0:T(8,128)} %rows_ref.1, s32[6,32]{1,0:T(8,128)} %cols_ref.1, bf16[2,2,768,768]{3,2,1,0:T(8,128)(2,1)} %constant.4.clone.wmid_hbm, bf16[2,2,384,192]{3,2,1,0:T(8,128)(2,1)} %constant.5.clone.wend_hbm), custom_call_target="tpu_custom_call" | custom-call | tf_op jit(solution)/shard_map/pallas_call | solution.py:532
  140.3 6.2 %copy.8 = f32[2,6,256,512]{3,2,1,0:T(8,128)} copy(f32[2,6,256,512]{3,2,1,0:T(8,128)} %bitcast.2) | data formatting | bytes 12582912
